TPU v7x, 32 devices: a whole 2x2x4 slice. The times are simulated.
32 devices in a mesh: dp: 4 (over z), row: 4 (over x, core), col: 2 (over y).
Axes of the slice: x: 2, y: 2, z: 4, core: 2. Of those that a mesh axis runs over, the one named last changes fastest.
Arguments:
- tokens: bfloat16 [16384, 1024], P(('dp', 'col'), 'row'), may hold values from -6 to 6
- lengths: int32 [16], P('dp'), may hold values from 128 to 1024, as said below
- qkv_weight: bfloat16 [1024, 3072], P('row', 'col'), may hold values from -0.1875 to 0.1875
- query_bias: float32 [1024], P('col'), may hold values from -4 to 4
- value_bias: float32 [1024], P('col'), may hold values from -0.75 to 0.75
- out_weight: bfloat16 [1024, 1024], P('col', 'row'), may hold values from -2 to 2
- out_bias: float32 [1024], P('row'), may hold values from -4 to 4
- first_norm_scale: float32 [1024], P('row'), may hold values from 0.5 to 1.5
- first_norm_bias: float32 [1024], P('row'), may hold values from -3 to 3
- up_weight: bfloat16 [1024, 4096], P('row', 'col'), may hold values from -0.1875 to 0.1875
- up_bias: float32 [4096], P('col'), may hold values from -4 to 4
- down_weight: bfloat16 [4096, 1024], P('col', 'row'), may hold values from -0.09375 to 0.09375
- down_bias: float32 [1024], P('row'), may hold values from -4 to 4
- second_norm_scale: float32 [1024], P('row'), may hold values from 0.5 to 1.5
- second_norm_bias: float32 [1024], P('row'), may hold values from -3 to 3
- cotangent: bfloat16 [16384, 1024], P(('dp', 'col'), 'row'), may hold values from -6 to 6
Outputs:
- layer_result_output: bfloat16 [16384, 1024], P(('dp', 'col'), 'row')
- grad_tokens: float32 [16384, 1024], P(('dp', 'col'), 'row')
- grad_qkv_weight: float32 [1024, 3072], P('row', 'col')
- grad_query_bias: float32 [1024], P('col')
- grad_value_bias: float32 [1024], P('col')
- grad_out_weight: float32 [1024, 1024], P('col', 'row')
- grad_out_bias: float32 [1024], P('row')
- grad_norm_one_gain: float32 [1024], P('row')
- grad_norm_one_shift: float32 [1024], P('row')
- grad_up_weight: float32 [1024, 4096], P('row', 'col')
- grad_up_bias: float32 [4096], P('col')
- grad_down_weight: float32 [4096, 1024], P('col', 'row')
- grad_down_bias: float32 [1024], P('row')
- grad_norm_two_gain: float32 [1024], P('row')
- grad_norm_two_shift: float32 [1024], P('row')
Inputs may be any that keep to these rules, and one draw needn't show every extreme that they name: `lengths`: valid tokens at the start of each sequence; keys at later positions are masked; in every draw some sequence has 1024 and some has 128.
All inputs are finite; a program needn't handle non-finite values.
Results may differ from a plain program's by a relative error of at most 0.012.
The roundings to bfloat16 on the way count: a program that leaves them out, or rounds other values in their place, can miss the bound.
Values may be sent and summed in bfloat16 or wider, within the bound.
A program may use at most 192 MiB of HBM per device.

v0:
```python
import jax
import jax.numpy as jnp
from jax import lax
from jax.sharding import PartitionSpec as P

HD = 64
LENGTH = 1024


norm_epsilon = 1e-12
masked_score = -1e30


def exact_gelu(values):
    return jax.nn.gelu(values, approximate=False)


def token_rows(values):
    return lax.all_gather(values, "col", axis=0, tiled=True)


def col_share(partials):
    return lax.psum_scatter(partials, "col", scatter_dimension=0, tiled=True)


def row_product(gathered, weight, contract):
    numbers = (((1,), (contract,)), ((), ()))
    return lax.psum_scatter(
        lax.dot_general(gathered, weight, numbers, preferred_element_type=jnp.float32),
        "row",
        scatter_dimension=0,
        tiled=True,
    )


def feature_rows(values, weight):
    return col_share(
        jnp.dot(
            lax.all_gather(values, "row", axis=0, tiled=True),
            weight,
            preferred_element_type=jnp.float32,
        )
    )


def weight_fold(values, gathered_grad):
    return lax.dot_general(
        lax.all_gather(values, "row", axis=0, tiled=True),
        gathered_grad,
        (((0,), (0,)), ((), ())),
        preferred_element_type=jnp.float32,
    )


def input_fold(grad_local, gathered_input, weight):
    shard_piece = lax.all_gather(grad_local, "row", axis=0, tiled=True)
    grad_weight = lax.dot_general(
        gathered_input, shard_piece, (((0,), (0,)), ((), ())), preferred_element_type=jnp.float32
    )
    product = lax.dot_general(
        shard_piece, weight, (((1,), (1,)), ((), ())), preferred_element_type=jnp.float32
    )
    return (product, grad_weight)


def row_pair(first_sum, second_sum):
    return lax.psum((first_sum, second_sum), "row")


def row_total(partial_sum):
    return lax.psum(partial_sum, "row")


def normalize_forward_pass(values, gain_vec, shift_vec):
    full_width = values.shape[1] * lax.axis_size("row")
    average = row_total(jnp.sum(values, axis=1)) / full_width
    centred = values - average[:, None]
    variance = row_total(jnp.sum(centred * centred, axis=1)) / full_width
    inverse = lax.rsqrt(variance + norm_epsilon)[:, None]
    normed = centred * inverse
    return (normed * gain_vec + shift_vec, normed, inverse)


def norm_backward(grad_out, normed, inverse, gain_vec):
    full_width = grad_out.shape[1] * lax.axis_size("row")
    scaled = grad_out * gain_vec
    first_sum, second_sum = row_pair(jnp.sum(scaled, axis=1), jnp.sum(scaled * normed, axis=1))
    grad_in = inverse * (
        scaled - first_sum[:, None] / full_width - normed * second_sum[:, None] / full_width
    )
    return (grad_in, jnp.sum(grad_out * normed, axis=0), jnp.sum(grad_out, axis=0))


def attend(query_part, key_part, value_part, length):
    seq_len = key_part.shape[0]
    heads_here = key_part.shape[1]
    block_rows = min(512, seq_len)
    score_scale = HD ** (-0.5)
    visible = (jnp.arange(seq_len) < length)[None, None, :]

    def one_block(query_block):
        scores = (
            jnp.einsum("qhd,khd->hqk", query_block, key_part, preferred_element_type=jnp.float32)
            * score_scale
        )
        scores = jnp.where(visible, scores, masked_score)
        highest = jnp.max(scores, axis=2, keepdims=True)
        weights = jnp.exp(scores - highest)
        totals = jnp.sum(weights, axis=2, keepdims=True)
        chances = (weights / totals).astype(jnp.bfloat16)
        context = jnp.einsum(
            "hqk,khd->qhd", chances, value_part, preferred_element_type=jnp.float32
        )
        return (context.astype(jnp.bfloat16), highest[:, :, 0] + jnp.log(totals[:, :, 0]))

    blocks = query_part.reshape(seq_len // block_rows, block_rows, heads_here, HD)
    contexts, log_sums = lax.map(one_block, blocks)
    return (contexts.reshape(seq_len, heads_here * HD), log_sums)


def attend_back(query_part, key_part, value_part, grad_context, log_sums, length):
    seq_len = key_part.shape[0]
    heads_here = key_part.shape[1]
    block_rows = min(512, seq_len)
    score_scale = HD ** (-0.5)
    visible = (jnp.arange(seq_len) < length)[None, None, :]

    def one_block(carried, inputs):
        grad_keys, grad_values = carried
        query_block, grad_block, block_sums = inputs
        scores = (
            jnp.einsum("qhd,khd->hqk", query_block, key_part, preferred_element_type=jnp.float32)
            * score_scale
        )
        scores = jnp.where(visible, scores, masked_score)
        chances = jnp.exp(scores - block_sums[:, :, None])
        grad_chances = jnp.einsum(
            "qhd,khd->hqk", grad_block, value_part, preferred_element_type=jnp.float32
        )
        inner_sum = jnp.sum(chances * grad_chances, axis=2, keepdims=True)
        grad_scores = (chances * (grad_chances - inner_sum)).astype(jnp.bfloat16)
        grad_query = (
            jnp.einsum("hqk,khd->qhd", grad_scores, key_part, preferred_element_type=jnp.float32)
            * score_scale
        )
        grad_keys = (
            grad_keys
            + jnp.einsum(
                "hqk,qhd->khd", grad_scores, query_block, preferred_element_type=jnp.float32
            )
            * score_scale
        )
        grad_values = grad_values + jnp.einsum(
            "hqk,qhd->khd",
            chances.astype(jnp.bfloat16),
            grad_block,
            preferred_element_type=jnp.float32,
        )
        return ((grad_keys, grad_values), grad_query)

    count_blocks = seq_len // block_rows
    query_blocks = query_part.reshape(count_blocks, block_rows, heads_here, HD)
    grad_blocks = grad_context.reshape(count_blocks, block_rows, heads_here, HD)
    zero_state = jnp.zeros(key_part.shape, jnp.float32)
    (grad_keys, grad_values), grad_queries = lax.scan(
        one_block, (zero_state, zero_state), (query_blocks, grad_blocks, log_sums)
    )
    return (grad_queries.reshape(seq_len, heads_here, HD), grad_keys, grad_values)


def widen_col(piece_vec):
    full_vec = jnp.zeros((piece_vec.shape[0] * lax.axis_size("col"),), jnp.float32)
    return lax.dynamic_update_slice_in_dim(
        full_vec, piece_vec, lax.axis_index("col") * piece_vec.shape[0], 0
    )


def widen_row(piece_vec):
    full_vec = jnp.zeros((piece_vec.shape[0] * lax.axis_size("row"),), jnp.float32)
    return lax.dynamic_update_slice_in_dim(
        full_vec, piece_vec, lax.axis_index("row") * piece_vec.shape[0], 0
    )


def narrow_col(full_vec, amount):
    return lax.dynamic_slice_in_dim(full_vec, lax.axis_index("col") * amount, amount, 0)


def narrow_row(full_vec, amount):
    return lax.dynamic_slice_in_dim(full_vec, lax.axis_index("row") * amount, amount, 0)


def shards(
    tokens,
    lengths,
    qkv_weight,
    query_bias,
    value_bias,
    out_weight,
    out_bias,
    first_norm_scale,
    first_norm_bias,
    up_weight,
    up_bias,
    down_weight,
    down_bias,
    second_norm_scale,
    second_norm_bias,
    cotangent,
):
    heads_here = qkv_weight.shape[1] // (3 * HD)
    length = lax.dynamic_index_in_dim(lengths, lax.axis_index("row"), 0, False)
    tokens_all = token_rows(tokens)
    mixed_qkv = row_product(tokens_all, qkv_weight, 0).reshape(LENGTH, heads_here, 3, HD)
    head_query = query_bias.reshape(heads_here, HD)
    heads_bias = jnp.stack(
        [head_query, jnp.zeros_like(head_query), value_bias.reshape(heads_here, HD)], axis=1
    )
    mixed_qkv = (mixed_qkv + heads_bias).astype(jnp.bfloat16)
    query_part = mixed_qkv[:, :, 0]
    key_part = mixed_qkv[:, :, 1]
    value_part = mixed_qkv[:, :, 2]
    context, log_sums = attend(query_part, key_part, value_part, length)
    first_residual = tokens.astype(jnp.float32) + feature_rows(context, out_weight) + out_bias
    first_normalized, first_standardized, first_inverse_deviation = normalize_forward_pass(
        first_residual, first_norm_scale, first_norm_bias
    )
    normed_all = token_rows(first_normalized.astype(jnp.bfloat16))
    upward = row_product(normed_all, up_weight, 0) + up_bias
    hidden_f, gelu_pull = jax.vjp(exact_gelu, upward)
    hidden = hidden_f.astype(jnp.bfloat16)
    second_residual = first_normalized + feature_rows(hidden, down_weight) + down_bias
    layer_result_output, second_standardized, second_inverse_deviation = normalize_forward_pass(
        second_residual, second_norm_scale, second_norm_bias
    )
    grad_resid_two, grad_gain_two, grad_shift_two = norm_backward(
        cotangent.astype(jnp.float32),
        second_standardized,
        second_inverse_deviation,
        second_norm_scale,
    )
    grad_down_bias = jnp.sum(grad_resid_two, axis=0)
    grad_down_all = token_rows(grad_resid_two.astype(jnp.bfloat16))
    grad_down_weight = weight_fold(hidden, grad_down_all)
    grad_hidden = row_product(grad_down_all, down_weight, 1)
    (grad_upward,) = gelu_pull(grad_hidden)
    grad_upward = grad_upward.astype(jnp.bfloat16)
    grad_up_bias = jnp.sum(grad_upward, axis=0, dtype=jnp.float32)
    back_up, grad_up_weight = input_fold(grad_upward, normed_all, up_weight)
    gradient_of_normalized = grad_resid_two + col_share(back_up)
    grad_resid_one, grad_gain_one, grad_shift_one = norm_backward(
        gradient_of_normalized, first_standardized, first_inverse_deviation, first_norm_scale
    )
    grad_out_bias = jnp.sum(grad_resid_one, axis=0)
    grad_attn_all = token_rows(grad_resid_one.astype(jnp.bfloat16))
    grad_out_weight = weight_fold(context, grad_attn_all)
    grad_context = row_product(grad_attn_all, out_weight, 1).astype(jnp.bfloat16)
    grad_context = grad_context.reshape(LENGTH, heads_here, HD)
    grad_queries, grad_keys, grad_values = attend_back(
        query_part, key_part, value_part, grad_context, log_sums, length
    )
    grad_mixed = jnp.stack([grad_queries, grad_keys, grad_values], axis=2).astype(jnp.bfloat16)
    head_sums = jnp.sum(grad_mixed, axis=0, dtype=jnp.float32)
    grad_query_bias = head_sums[:, 0].reshape(heads_here * HD)
    grad_value_bias = head_sums[:, 2].reshape(heads_here * HD)
    back_qkv, grad_qkv_weight = input_fold(
        grad_mixed.reshape(LENGTH, heads_here * 3 * HD), tokens_all, qkv_weight
    )
    grad_tokens = grad_resid_one + col_share(back_qkv)
    col_width = grad_query_bias.shape[0]
    up_width = grad_up_bias.shape[0]
    row_width = grad_out_bias.shape[0]
    (
        wide_query,
        wide_value,
        wide_up,
        wide_out,
        wide_gain_one,
        wide_shift_one,
        wide_down,
        wide_gain_two,
        wide_shift_two,
    ) = lax.psum(
        (
            widen_col(grad_query_bias),
            widen_col(grad_value_bias),
            widen_col(grad_up_bias),
            widen_row(grad_out_bias),
            widen_row(grad_gain_one),
            widen_row(grad_shift_one),
            widen_row(grad_down_bias),
            widen_row(grad_gain_two),
            widen_row(grad_shift_two),
        ),
        ("row", "col"),
    )
    summed = lax.psum(
        (
            grad_qkv_weight,
            narrow_col(wide_query, col_width),
            narrow_col(wide_value, col_width),
            grad_out_weight,
            narrow_row(wide_out, row_width),
            narrow_row(wide_gain_one, row_width),
            narrow_row(wide_shift_one, row_width),
            grad_up_weight,
            narrow_col(wide_up, up_width),
            grad_down_weight,
            narrow_row(wide_down, row_width),
            narrow_row(wide_gain_two, row_width),
            narrow_row(wide_shift_two, row_width),
        ),
        "dp",
    )
    return (
        layer_result_output.astype(jnp.bfloat16),
        grad_tokens,
        summed[0],
        summed[1],
        summed[2],
        summed[3],
        summed[4],
        summed[5],
        summed[6],
        summed[7],
        summed[8],
        summed[9],
        summed[10],
        summed[11],
        summed[12],
    )


def solution(mesh):
    placed = (
        P(("dp", "col"), "row"),
        P("dp"),
        P("row", "col"),
        P("col"),
        P("col"),
        P("col", "row"),
        P("row"),
        P("row"),
        P("row"),
        P("row", "col"),
        P("col"),
        P("col", "row"),
        P("row"),
        P("row"),
        P("row"),
        P(("dp", "col"), "row"),
    )
    return jax.shard_map(
        shards,
        mesh=mesh,
        in_specs=placed,
        out_specs=(
            P(("dp", "col"), "row"),
            P(("dp", "col"), "row"),
            P("row", "col"),
            P("col"),
            P("col"),
            P("col", "row"),
            P("row"),
            P("row"),
            P("row"),
            P("row", "col"),
            P("col"),
            P("col", "row"),
            P("row"),
            P("row"),
            P("row"),
        ),
        check_vma=False,
    )
```

profile of v0, /device:TPU:0, one launch (start us, length us, event | category | flops | bytes accessed | tf_op | source)
XLA Modules:
  0.0 2028.0 jit_solution(9098031321460476217)
XLA Ops:
  8.0 37.4 %all-gather.9.cloned.1.call-done = bf16[4096,256]{1,0:T(8,128)(2,1)} async-done(((bf16[2048,256]{1,0:T(8,128)(2,1)}), bf16[4096,256]{1,0:T(8,128)(2,1)}) %all-gather.9.cloned.1.call-update) | async-done | bytes 2097168 | tf_op jit(solution)/shard_map/all_gather | solution.py:19
  60.5 179.0 %reduce-scatter.9.cloned.1.call-done = f32[1024,1536]{1,0:T(8,128)} async-done(((f32[4096,1536]{1,0:T(8,128)}), f32[1024,1536]{1,0:T(8,128)}) %reduce-scatter.9.cloned.1.call-update) | async-done | bytes 6291472 | tf_op jit(solution)/shard_map/reduce_scatter | solution.py:28
  253.0 29.9 %while.28 = (s32[]{:T(128)}, bf16[2,512,8,64]{1,3,2,0:T(8,128)(2,1)}, f32[2,8,512]{2,1,0:T(8,128)S(1)}, bf16[2,512,8,64]{1,3,2,0:T(8,128)(2,1)}, bf16[1024,8,64]...) while((s32[]{:T(128)}, bf16[2,512,8,64]{1,3,2,0:T(8,128)(2,1)}, ...), condition=%wide.region_4.5_spmd.clone, body=%wide.region_1.4_spmd.clone.sunk | while | flops 1124332544 | bytes 62001316 | solution.py:117
  286.5 34.6 %all-gather.11.cloned.1.call-done = bf16[4096,512]{0,1:T(8,128)(2,1)} async-done(((bf16[1024,512]{0,1:T(8,128)(2,1)}), bf16[4096,512]{0,1:T(8,128)(2,1)}) %all-gather.11.cloned.1.call-update) | async-done | bytes 4194320 | tf_op jit(solution)/shard_map/all_gather | solution.py:39
  326.6 54.4 %reduce-scatter.11.cloned.1.call-done = f32[2048,256]{1,0:T(8,128)} async-done(((f32[4096,256]{1,0:T(8,128)}), f32[2048,256]{1,0:T(8,128)}) %reduce-scatter.11.cloned.1.call-update) | async-done | bytes 2097168 | tf_op jit(solution)/shard_map/reduce_scatter | solution.py:23
  399.0 31.9 %all-gather.13.cloned.1.call-done = bf16[4096,256]{1,0:T(8,128)(2,1)} async-done(((bf16[2048,256]{1,0:T(8,128)(2,1)}), bf16[4096,256]{1,0:T(8,128)(2,1)}) %all-gather.13.cloned.1.call-update) | async-done | bytes 2097168 | tf_op jit(solution)/shard_map/all_gather | solution.py:19
  448.4 235.1 %reduce-scatter.13.cloned.1.call-done = f32[1024,2048]{1,0:T(8,128)} async-done(((f32[4096,2048]{1,0:T(8,128)}), f32[1024,2048]{1,0:T(8,128)}) %reduce-scatter.13.cloned.1.call-update) | async-done | bytes 8388624 | tf_op jit(solution)/shard_map/reduce_scatter | solution.py:28
  683.5 21.0 %multiply_convert_fusion.1 = (bf16[1024,2048]{1,0:T(8,128)(2,1)}, f32[1024,2048]{1,0:T(8,128)}) fusion(f32[1024,2048]{1,0:T(8,128)} %reduce-scatter.13.cloned.1.call-done, f32[2048]{0:T(1024)S(1)} %copy-done.20), kind=kLoop, calls=%fused_computation.47 | loop fusion | flops 138412032 | bytes 20979712 | tf_op jit(solution)/shard_map/convert_element_type | solution.py:231
  704.6 106.0 %all-gather.15.cloned.1.call-done = bf16[4096,2048]{1,0:T(8,128)(2,1)} async-done(((bf16[1024,2048]{1,0:T(8,128)(2,1)}), bf16[4096,2048]{1,0:T(8,128)(2,1)}) %all-gather.15.cloned.1.call-update) | async-done | bytes 16777232 | tf_op jit(solution)/shard_map/all_gather | solution.py:39
  820.8 54.4 %reduce-scatter.15.cloned.1.call-done = f32[2048,256]{1,0:T(8,128)} async-done(((f32[4096,256]{1,0:T(8,128)}), f32[2048,256]{1,0:T(8,128)}) %reduce-scatter.15.cloned.1.call-update) | async-done | bytes 2097168 | tf_op jit(solution)/shard_map/reduce_scatter | solution.py:23
  914.5 32.8 %all-gather.17.cloned.1.call-done = bf16[4096,256]{1,0:T(8,128)(2,1)} async-done(((bf16[2048,256]{1,0:T(8,128)(2,1)}), bf16[4096,256]{1,0:T(8,128)(2,1)}) %all-gather.17.cloned.1.call-update) | async-done | bytes 2097168 | tf_op jit(solution)/shard_map/all_gather | solution.py:19
  962.1 234.9 %reduce-scatter.17.cloned.1.call-done = f32[1024,2048]{1,0:T(8,128)} async-done(((f32[4096,2048]{1,0:T(8,128)}), f32[1024,2048]{1,0:T(8,128)}) %reduce-scatter.17.cloned.1.call-update) | async-done | bytes 8388624 | tf_op jit(solution)/shard_map/reduce_scatter | solution.py:28
  1210.1 106.0 %all-gather.19.cloned.1.call-done = bf16[4096,2048]{1,0:T(8,128)(2,1)} async-done(((bf16[1024,2048]{1,0:T(8,128)(2,1)}), bf16[4096,2048]{1,0:T(8,128)(2,1)}) %all-gather.19.cloned.1.call-update) | async-done | bytes 16777232 | tf_op jit(solution)/shard_map/all_gather | solution.py:56
  1326.3 54.4 %reduce-scatter.19.cloned.1.call-done = f32[2048,256]{1,0:T(8,128)} async-done(((f32[4096,256]{1,0:T(8,128)}), f32[2048,256]{1,0:T(8,128)}) %reduce-scatter.19.cloned.1.call-update) | async-done | bytes 2097168 | tf_op jit(solution)/shard_map/reduce_scatter | solution.py:23
  1402.5 32.3 %all-gather.21.cloned.1.call-done = bf16[4096,256]{1,0:T(8,128)(2,1)} async-done(((bf16[2048,256]{1,0:T(8,128)(2,1)}), bf16[4096,256]{1,0:T(8,128)(2,1)}) %all-gather.21.cloned.1.call-update) | async-done | bytes 2097168 | tf_op jit(solution)/shard_map/all_gather | solution.py:19
  1441.0 71.8 %reduce-scatter.21.cloned.1.call-done = f32[1024,512]{1,0:T(8,128)} async-done(((f32[4096,512]{1,0:T(8,128)}), f32[1024,512]{1,0:T(8,128)}) %reduce-scatter.21.cloned.1.call-update) | async-done | bytes 2097168 | tf_op jit(solution)/shard_map/reduce_scatter | solution.py:28
  1518.1 119.2 %while.29 = (s32[]{:T(128)}, f32[1024,8,64]{0,2,1:T(8,128)}, f32[1024,8,64]{0,2,1:T(8,128)}, bf16[2,512,8,64]{1,0,3,2:T(2,128)(2,1)}, bf16[2,512,8,64]{1,3,2,0:T...) while((s32[]{:T(128)}, f32[1024,8,64]{0,2,1:T(8,128)}, ...), condition=%wide.region_29.30_spmd.clone, body=%wide.region_27.29_spmd.clone.sunk | while | flops 2725245952 | bytes 192497904 | solution.py:165
  1559.1 18.3 dynamic_update_slice.58
  1619.0 18.3 dynamic_update_slice.58
  1670.1 56.3 %all-gather.23.cloned.1.call-done = bf16[4096,1536]{0,1:T(8,128)(2,1)} async-done(((bf16[1024,1536]{0,1:T(8,128)(2,1)}), bf16[4096,1536]{0,1:T(8,128)(2,1)}) %all-gather.23.cloned.1.call-update) | async-done | bytes 12582928 | tf_op jit(solution)/shard_map/all_gather | solution.py:56
  1747.6 25.6 %all-reduce = (f32[1024]{0:T(1024)S(1)}, f32[1024]{0:T(1024)S(1)}, f32[1024]{0:T(1024)S(1)}, f32[1024]{0:T(1024)S(1)}, f32[1024]{0:T(1024)S(1)}, /*index=5*/f32[...) all-reduce(f32[1024]{0:T(1024)S(1)} %dynamic_update_slice.39, ...), channel_id=1, replica_groups=mesh['dp'=4,'row'=4,'col'=2] {'row','col'}, use_global_device_ids=true, to_apply=%region_33.34 | all-reduce | flops 12288 | bytes 98304 | tf_op jit(solution)/shard_map/psum | solution.py:283
  1773.9 24.8 %all-reduce.3 = (f32[512]{0:T(512)}, f32[512]{0:T(512)}, f32[256]{0:T(256)}, f32[256]{0:T(256)}, f32[256]{0:T(256)}, /*index=5*/f32[2048]{0:T(1024)}, f32[256]{0:T(256)}, f32[256]{0:T(256)}, f32[256]{0:T(256)}) all-reduce(f32[512]{0:T(512)S(1)} %dynamic_slice.46, ...), channel_id=1, replica_groups=mesh['dp'=4,'row'=4,'col'=2] {'dp'}, use_global_device_ids=true, to_apply=%region_34.35 | all-reduce | flops 4608 | bytes 36864 | tf_op jit(solution)/shard_map/psum | solution.py:297
  1798.7 160.4 %all-reduce.7.cloned.1.call-done = (f32[256,1536]{0,1:T(8,128)}, f32[512,256]{1,0:T(8,128)}, f32[256,2048]{1,0:T(8,128)}, f32[2048,256]{1,0:T(8,128)}) async-done(((f32[256,1536]{0,1:T(8,128)}, f32[512,256]{1,0:T(8,128)}, f32[256,2048]{1,0:T(8,128)}, f32[2048,256]{1,0:T(8,128)}), (f32[256,1536]{0,1:T(8,128)}, f32[512,256]{1,0:T(8,128)}, f32[256,2048]{1,0:T(8,128)}, ...) | async-done | bytes 6291472 | tf_op jit(solution)/shard_map/psum | solution.py:297
  1962.0 52.4 %reduce-scatter.23.cloned.1.call-done = f32[2048,256]{1,0:T(8,128)} async-done(((f32[4096,256]{1,0:T(8,128)}), f32[2048,256]{1,0:T(8,128)}) %reduce-scatter.23.cloned.1.call-update) | async-done | bytes 2097168 | tf_op jit(solution)/shard_map/reduce_scatter | solution.py:23
  (240 shorter events, 371.1 us)
Async XLA Ops:
  7.2 803.4 %copy-start = (bf16[2048,256]{1,0:T(8,128)(2,1)S(1)}, bf16[2048,256]{1,0:T(8,128)(2,1)}, u32[]{:S(2)}) copy-start(bf16[2048,256]{1,0:T(8,128)(2,1)} %param.31) | copy-start | bytes 3145732
  7.2 38.2 %all-gather.9.cloned.1.call-start = ((), (), s32[]{:S(2)}) async-start(), calls=%async_computation.8 | async-start | bytes 3145728 | tf_op jit(solution)/shard_map/all_gather | solution.py:19
  7.9 231.6 %reduce-scatter.9.cloned.1.call-start = ((), (), s32[]{:S(2)}) async-start(), calls=%async_computation.9 | async-start | bytes 31457280 | tf_op jit(solution)/shard_map/reduce_scatter | solution.py:28
  59.0 262.1 %all-gather.11.cloned.1.call-start = ((), (), s32[]{:S(2)}) async-start(), calls=%async_computation.10 | async-start | bytes 5242880 | tf_op jit(solution)/shard_map/all_gather | solution.py:39
  286.4 94.6 %copy-start.35 = (f32[256]{0:T(256)S(1)}, f32[256]{0:T(256)}, u32[]{:S(2)}) copy-start(f32[256]{0:T(256)} %param.26) | copy-start | bytes 3076
  286.4 94.5 %reduce-scatter.11.cloned.1.call-start = ((), (), s32[]{:S(2)}) async-start(), calls=%async_computation.11 | async-start | bytes 6291456 | tf_op jit(solution)/shard_map/reduce_scatter | solution.py:23
  326.5 104.4 %all-gather.13.cloned.1.call-start = ((), (), s32[]{:S(2)}) async-start(), calls=%async_computation.12 | async-start | bytes 3145728 | tf_op jit(solution)/shard_map/all_gather | solution.py:19
  398.5 285.1 %reduce-scatter.13.cloned.1.call-start = ((), (), s32[]{:S(2)}) async-start(), calls=%async_computation.13 | async-start | bytes 41943040 | tf_op jit(solution)/shard_map/reduce_scatter | solution.py:28
  448.4 235.2 %copy-start.20 = (f32[2048]{0:T(1024)S(1)}, f32[2048]{0:T(1024)}, u32[]{:S(2)}) copy-start(f32[2048]{0:T(1024)} %param.30) | copy-start | bytes 24580
  448.4 362.2 %all-gather.15.cloned.1.call-start = ((), (), s32[]{:S(2)}) async-start(), calls=%async_computation.14 | async-start | bytes 20971520 | tf_op jit(solution)/shard_map/all_gather | solution.py:39
  704.5 170.7 %copy-start.33 = (f32[256]{0:T(256)S(1)}, f32[256]{0:T(256)}, u32[]{:S(2)}) copy-start(f32[256]{0:T(256)} %param.32) | copy-start | bytes 3076
  704.5 170.7 %reduce-scatter.15.cloned.1.call-start = ((), (), s32[]{:S(2)}) async-start(), calls=%async_computation.15 | async-start | bytes 6291456 | tf_op jit(solution)/shard_map/reduce_scatter | solution.py:23
  820.7 86.5 %copy-start.34 = (f32[256]{0:T(256)S(1)}, f32[256]{0:T(256)}, u32[]{:S(2)}) copy-start(f32[256]{0:T(256)} %param.34) | copy-start | bytes 3076
  820.7 126.6 %all-gather.17.cloned.1.call-start = ((), (), s32[]{:S(2)}) async-start(), calls=%async_computation.16 | async-start | bytes 3145728 | tf_op jit(solution)/shard_map/all_gather | solution.py:19
  914.5 282.6 %reduce-scatter.17.cloned.1.call-start = ((), (), s32[]{:S(2)}) async-start(), calls=%async_computation.17 | async-start | bytes 41943040 | tf_op jit(solution)/shard_map/reduce_scatter | solution.py:28
  962.0 354.1 %all-gather.19.cloned.1.call-start = ((), (), s32[]{:S(2)}) async-start(), calls=%async_computation.18 | async-start | bytes 20971520 | tf_op jit(solution)/shard_map/all_gather | solution.py:56
  1197.0 119.1 %copy-start.14 = (bf16[256,2048]{1,0:T(8,128)(2,1)S(1)}, bf16[256,2048]{1,0:T(8,128)(2,1)}, u32[]{:S(2)}) copy-start(bf16[256,2048]{1,0:T(8,128)(2,1)} %param.29) | copy-start | bytes 3145732
  1210.0 170.7 %reduce-scatter.19.cloned.1.call-start = ((), (), s32[]{:S(2)}) async-start(), calls=%async_computation.19 | async-start | bytes 6291456 | tf_op jit(solution)/shard_map/reduce_scatter | solution.py:23
  1326.2 108.5 %all-gather.21.cloned.1.call-start = ((), (), s32[]{:S(2)}) async-start(), calls=%async_computation.20 | async-start | bytes 3145728 | tf_op jit(solution)/shard_map/all_gather | solution.py:19
  1402.4 110.4 %reduce-scatter.21.cloned.1.call-start = ((), (), s32[]{:S(2)}) async-start(), calls=%async_computation.21 | async-start | bytes 10485760 | tf_op jit(solution)/shard_map/reduce_scatter | solution.py:28
  1440.9 285.4 %all-gather.23.cloned.1.call-start = ((), (), s32[]{:S(2)}) async-start(), calls=%async_computation.22 | async-start | bytes 15728640 | tf_op jit(solution)/shard_map/all_gather | solution.py:56
  1644.1 314.9 %all-reduce.7.cloned.1.call-start = ((), (), s32[]{:S(2)}) async-start(), calls=%async_computation.24 | async-start | bytes 12582912 | tf_op jit(solution)/shard_map/psum | solution.py:297
  1734.0 280.5 %reduce-scatter.23.cloned.1.call-start = ((), (), s32[]{:S(2)}) async-start(), calls=%async_computation.23 | async-start | bytes 6291456 | tf_op jit(solution)/shard_map/reduce_scatter | solution.py:23
  1745.3 269.2 %copy-start.6 = (f32[2048,256]{1,0:T(8,128)S(1)}, f32[2048,256]{1,0:T(8,128)}, u32[]{:S(2)}) copy-start(f32[2048,256]{1,0:T(8,128)} %copy-done.5) | copy-start | bytes 6291460
  (35 other events, 560.6 us)
Sparse Core Ops, SparseCore 0:
  9.6 35.8 all-gather.8
  59.1 180.4 reduce-scatter.8
  286.6 34.4 all-gather.10
  326.6 54.3 reduce-scatter.10
  398.6 32.2 all-gather.12
  448.5 234.9 reduce-scatter.12
  704.6 105.9 all-gather.14
  820.8 54.3 reduce-scatter.14
  914.6 32.7 all-gather.16
  962.2 234.8 reduce-scatter.16
  1210.2 105.9 all-gather.18
  1326.4 54.3 reduce-scatter.18
  1402.5 32.1 all-gather.20
  1441.0 71.7 reduce-scatter.20
  1644.2 82.0 all-gather.22
  1734.0 224.9 all-reduce.6
  1961.3 53.1 reduce-scatter.22
where the time goes:
time: 2040 us; the launch traced here: 2030 us
  waiting for transfers between devices  1540 us (75%)
  matrix products  200 us (10%)
  other arithmetic  102 us (5%)
  blocking collectives  98 us (5%)
  local copies, waits for them, and re-layouts  75.9 us (4%)
    reduce_scatter x4, waiting for transfers between devices, row_product(): lax.psum_scatter(lax.dot_general(gathered, weight, numbers, preferred_ele...  721 us
    reduce_scatter x4, waiting for transfers between devices, col_share(): return lax.psum_scatter(partials, 'col', scatter_dimension=0, tiled=True)  216 us
    all_gather x2, waiting for transfers between devices, input_fold(): shard_piece = lax.all_gather(grad_local, 'row', axis=0, tiled=True)  162 us
    psum x1, waiting for transfers between devices, shards(): lax.psum((grad_qkv_weight, narrow_col(wide_query, col_width), narrow_col(...  160 us
    all_gather x2, waiting for transfers between devices, feature_rows(): lax.all_gather(values, 'row', axis=0, tiled=True)  141 us
    all_gather x4, waiting for transfers between devices, token_rows(): return lax.all_gather(values, 'col', axis=0, tiled=True)  134 us
    dot_general x4, matrix products, row_product(): lax.dot_general(gathered, weight, numbers, preferred_element_type=jnp.flo...  51.7 us
  transfers between devices with their start and end apart: 17, of which 17 were waited for; matrix products, arithmetic and copies ran while one was open for 2% of the time, Pallas kernels for 0%

commit v1 on v0

v1 whole, which is shorter than its diff:
```python
import jax
import jax.numpy as jnp
from jax import lax
from jax.experimental import pallas as pl
from jax.experimental.pallas import tpu as pltpu
from jax.sharding import Mesh, PartitionSpec as P

HD = 64
LENGTH = 1024
QUERY_BLOCK = 256

norm_epsilon = 1e-12
masked_score = -1e30
F32 = jnp.float32
BF16 = jnp.bfloat16


def swap(values, axis):
    return lax.ppermute(values, axis, [(0, 1), (1, 0)])


def pick(values, index, amount):
    return lax.dynamic_slice_in_dim(values, index * amount, amount, 0)


def in_order(index, mine, other, axis=0):
    return jnp.where(
        index == 0,
        jnp.concatenate([mine, other], axis=axis),
        jnp.concatenate([other, mine], axis=axis),
    )


def dot(left, right, contract=((1,), (0,))):
    return lax.dot_general(left, right, (contract, ((), ())), preferred_element_type=F32)


def gather_plane(first, second):
    first_x = swap(first, "x")
    second_y = swap(second, "col")
    first_y = swap(first, "col")
    second_x = swap(second, "x")
    first_xy = swap(first_x, "col")
    second_xy = swap(second_y, "x")
    return (
        [[first, first_y], [first_x, first_xy]],
        [[second, second_y], [second_x, second_xy]],
    )


def scatter_plane(first, second):
    def go(blocks, axes):
        near = blocks[0][0].astype(F32) + swap(blocks[0][1], axes[0]).astype(F32)
        far = blocks[1][0].astype(F32) + swap(blocks[1][1], axes[0]).astype(F32)
        return near + swap(far.astype(BF16), axes[1]).astype(F32)

    turned = [[second[0][0], second[1][0]], [second[0][1], second[1][1]]]
    return go(first, ("col", "x")), go(turned, ("x", "col"))


def over_groups(values, after):
    values = tuple(value.astype(BF16) for value in values)
    if after is not None:
        values, after = lax.optimization_barrier((values, after))
    return lax.psum(values, "dp")


def gather_core(values):
    return jnp.concatenate([values, swap(values, "core")], axis=0)


def reduce_core(partials):
    half = partials.shape[0] // 2
    return partials[:half] + swap(partials[half:], "core")


def attend_body(place_ref, mixed_ref, context_ref, sums_ref):
    length = place_ref[0]
    offset = place_ref[1]
    count = mixed_ref.shape[0]
    position = lax.broadcasted_iota(jnp.int32, (count, 1), 0) + offset
    position = jnp.where(position >= count, position - count, position)
    visible = position < length
    for block in range(count // QUERY_BLOCK):
        rows = pl.ds(block * QUERY_BLOCK, QUERY_BLOCK)
        parts = []
        for head in range(2):
            start = head * 3 * HD
            query = mixed_ref[rows, start : start + HD] * jnp.asarray(HD ** (-0.5), BF16)
            key = mixed_ref[:, start + HD : start + 2 * HD]
            value = mixed_ref[:, start + 2 * HD : start + 3 * HD]
            scores = jnp.where(visible, dot(key, query, ((1,), (1,))), masked_score)
            highest = jnp.max(scores, axis=0, keepdims=True)
            weights = jnp.exp(scores - highest)
            totals = jnp.sum(weights, axis=0, keepdims=True)
            chances = (weights * (1.0 / totals)).astype(BF16)
            parts.append(dot(value, chances, ((0,), (0,))))
            sums_ref[0, head : head + 1, rows] = highest + jnp.log(totals)
        context_ref[rows, :] = jnp.concatenate(parts, axis=0).T.astype(BF16)


def attend(mixed, place):
    count = mixed.shape[0]
    pairs = mixed.shape[1] // (6 * HD)
    return pl.pallas_call(
        attend_body,
        grid=(pairs,),
        in_specs=[
            pl.BlockSpec(memory_space=pltpu.SMEM),
            pl.BlockSpec((count, 6 * HD), lambda pair: (0, pair)),
        ],
        out_specs=[
            pl.BlockSpec((count, 2 * HD), lambda pair: (0, pair)),
            pl.BlockSpec((1, 2, count), lambda pair: (pair, 0, 0)),
        ],
        out_shape=[
            jax.ShapeDtypeStruct((count, pairs * 2 * HD), BF16),
            jax.ShapeDtypeStruct((pairs, 2, count), F32),
        ],
        compiler_params=pltpu.CompilerParams(vmem_limit_bytes=40 * 2**20),
        cost_estimate=pl.CostEstimate(
            flops=pairs * 8 * count * count * HD,
            bytes_accessed=mixed.size * 3,
            transcendentals=pairs * 2 * count * count,
        ),
        name="attend",
    )(place, mixed)


def attend_back_body(place_ref, mixed_ref, grad_ref, sums_ref, out_ref):
    length = place_ref[0]
    offset = place_ref[1]
    count = mixed_ref.shape[0]
    position = lax.broadcasted_iota(jnp.int32, (count, 1), 0) + offset
    position = jnp.where(position >= count, position - count, position)
    visible = position < length
    scale = HD ** (-0.5)
    for head in range(2):
        start = head * 3 * HD
        key = mixed_ref[:, start + HD : start + 2 * HD]
        value = mixed_ref[:, start + 2 * HD : start + 3 * HD]
        grad_key = jnp.zeros((count, HD), F32)
        grad_value = jnp.zeros((count, HD), F32)
        for block in range(count // QUERY_BLOCK):
            rows = pl.ds(block * QUERY_BLOCK, QUERY_BLOCK)
            query = mixed_ref[rows, start : start + HD] * jnp.asarray(scale, BF16)
            grad = grad_ref[rows, head * HD : (head + 1) * HD]
            scores = jnp.where(visible, dot(key, query, ((1,), (1,))), masked_score)
            chances = jnp.exp(scores - sums_ref[0, head : head + 1, rows])
            grad_chances = dot(value, grad, ((1,), (1,)))
            inner = jnp.sum(chances * grad_chances, axis=0, keepdims=True)
            grad_scores = (chances * (grad_chances - inner)).astype(BF16)
            grad_value += dot(chances.astype(BF16), grad)
            grad_key += dot(grad_scores, query)
            grad_query = dot(key, grad_scores, ((0,), (0,))) * scale
            out_ref[rows, start : start + HD] = grad_query.T.astype(BF16)
        out_ref[:, start + HD : start + 2 * HD] = grad_key.astype(BF16)
        out_ref[:, start + 2 * HD : start + 3 * HD] = grad_value.astype(BF16)


def attend_back(mixed, grad_context, log_sums, place):
    count = mixed.shape[0]
    pairs = mixed.shape[1] // (6 * HD)
    return pl.pallas_call(
        attend_back_body,
        grid=(pairs,),
        in_specs=[
            pl.BlockSpec(memory_space=pltpu.SMEM),
            pl.BlockSpec((count, 6 * HD), lambda pair: (0, pair)),
            pl.BlockSpec((count, 2 * HD), lambda pair: (0, pair)),
            pl.BlockSpec((1, 2, count), lambda pair: (pair, 0, 0)),
        ],
        out_specs=pl.BlockSpec((count, 6 * HD), lambda pair: (0, pair)),
        out_shape=jax.ShapeDtypeStruct(mixed.shape, BF16),
        compiler_params=pltpu.CompilerParams(vmem_limit_bytes=40 * 2**20),
        cost_estimate=pl.CostEstimate(
            flops=pairs * 20 * count * count * HD,
            bytes_accessed=mixed.size * 5,
            transcendentals=pairs * 2 * count * count,
        ),
        name="attend_back",
    )(place, mixed, grad_context, log_sums)


def normalize(values, gain_vec, shift_vec):
    average = jnp.mean(values, axis=1, keepdims=True)
    centred = values - average
    variance = jnp.mean(centred * centred, axis=1, keepdims=True)
    inverse = lax.rsqrt(variance + norm_epsilon)
    normed = centred * inverse
    return normed * gain_vec + shift_vec, normed, inverse


def normalize_back(grad_out, normed, inverse, gain_vec):
    scaled = grad_out * gain_vec
    grad_in = inverse * (
        scaled
        - jnp.mean(scaled, axis=1, keepdims=True)
        - normed * jnp.mean(scaled * normed, axis=1, keepdims=True)
    )
    return grad_in, jnp.sum(grad_out * normed, axis=0), jnp.sum(grad_out, axis=0)


def shards(
    tokens,
    lengths,
    qkv_weight,
    query_bias,
    value_bias,
    out_weight,
    out_bias,
    first_norm_scale,
    first_norm_bias,
    up_weight,
    up_bias,
    down_weight,
    down_bias,
    second_norm_scale,
    second_norm_bias,
    cotangent,
):
    x = lax.axis_index("x")
    core = lax.axis_index("core")
    col = lax.axis_index("col")
    width = tokens.shape[1]
    half = LENGTH // 2
    place = jnp.stack(
        [lax.dynamic_index_in_dim(lengths, 2 * col + x, 0, False), core * half]
    ).astype(jnp.int32)

    def by_core(mine, other):
        return jnp.where(core == 0, mine, other), jnp.where(core == 0, other, mine)

    def pair_columns(values):
        mine = pick(values, x, LENGTH)
        other = swap(pick(values, 1 - x, LENGTH), "x")
        return jnp.concatenate([mine, other], axis=1)

    def spread(parts):
        mine, other = by_core(*parts)
        return jnp.concatenate(
            [
                mine[:, :width],
                other[:, :width],
                mine[:, width:],
                other[:, width:],
            ],
            axis=1,
        )

    token_pair = pair_columns(tokens)
    token_pair = jnp.concatenate(
        [pick(token_pair, core, half), pick(token_pair, 1 - core, half)], axis=0
    )
    came = swap(token_pair, "core")
    came = jnp.concatenate([came[half:], came[:half]], axis=0)
    tokens_all = spread((token_pair, came))

    def column_share(weight):
        amount = weight.shape[1] // 2
        mine = lax.dynamic_slice_in_dim(weight, core * amount, amount, 1)
        other = swap(lax.dynamic_slice_in_dim(weight, (1 - core) * amount, amount, 1), "core")
        return by_core(mine, other)

    def row_share(weight):
        amount = weight.shape[0] // 2
        return by_core(
            pick(weight, core, amount), swap(pick(weight, 1 - core, amount), "core")
        )

    def full_rows(halves):
        first, second = halves
        return jnp.concatenate(
            [
                jnp.concatenate(blocks, axis=1)
                for blocks in (first[0], second[0], first[1], second[1])
            ],
            axis=0,
        )

    def full_columns(halves):
        first, second = halves
        return jnp.concatenate(
            [
                jnp.concatenate(
                    [first[0][side], second[0][side], first[1][side], second[1][side]], axis=1
                )
                for side in range(2)
            ],
            axis=0,
        )

    qkv_full = full_rows(gather_plane(*column_share(qkv_weight)))
    out_full = full_columns(gather_plane(*row_share(out_weight)))
    up_full = full_rows(gather_plane(*column_share(up_weight)))
    down_full = full_columns(gather_plane(*row_share(down_weight)))

    row_vectors = lax.all_gather(
        jnp.stack(
            [
                out_bias,
                first_norm_scale,
                first_norm_bias,
                down_bias,
                second_norm_scale,
                second_norm_bias,
            ]
        ),
        ("x", "core"),
        axis=0,
    )
    count = row_vectors.shape[1]

    def turn(blocks, axis_index, axis):
        return jnp.where(axis_index == 0, blocks, jnp.flip(blocks, axis))

    row_vectors = row_vectors.reshape(2, 2, count, width)
    row_vectors = turn(row_vectors, x, 0)
    row_vectors = row_vectors.transpose(2, 0, 1, 3).reshape(count, 4 * width)
    out_bias_all, gain_one, shift_one, down_bias_all, gain_two, shift_two = [
        row_vectors[index] for index in range(count)
    ]
    head_amount = query_bias.shape[0]
    up_amount = up_bias.shape[0]
    col_vectors = lax.all_gather(
        jnp.concatenate([query_bias, value_bias, up_bias]), "col", axis=0
    )
    col_vectors = turn(col_vectors, col, 0)

    def core_columns(values):
        amount = values.shape[1] // 2
        return lax.dynamic_slice_in_dim(values, core * amount, amount, 1)

    query_bias_here = core_columns(col_vectors[:, :head_amount]).reshape(-1, HD)
    value_bias_here = core_columns(col_vectors[:, head_amount : 2 * head_amount]).reshape(-1, HD)
    up_bias_here = core_columns(col_vectors[:, 2 * head_amount :]).reshape(-1)
    heads_bias = jnp.stack(
        [query_bias_here, jnp.zeros_like(query_bias_here), value_bias_here], axis=1
    ).reshape(-1)

    mixed = (dot(tokens_all, qkv_full) + heads_bias).astype(BF16)
    context, log_sums = attend(mixed, place)
    tokens_here = tokens_all[:half].astype(F32)
    first_residual = tokens_here + reduce_core(dot(context, out_full)) + out_bias_all
    first_normalized, first_standardized, first_inverse = normalize(
        first_residual, gain_one, shift_one
    )
    normed_all = gather_core(first_normalized.astype(BF16))
    upward = dot(normed_all, up_full) + up_bias_here
    hidden_f, gelu_pull = jax.vjp(
        lambda values: jax.nn.gelu(values, approximate=False), upward
    )
    hidden = hidden_f.astype(BF16)
    second_residual = first_normalized + reduce_core(dot(hidden, down_full)) + down_bias_all
    layer_result, second_standardized, second_inverse = normalize(
        second_residual, gain_two, shift_two
    )

    def hand_back(values):
        kept, sent = by_core(
            jnp.concatenate([values[:, :width], values[:, 2 * width : 3 * width]], axis=1),
            jnp.concatenate([values[:, width : 2 * width], values[:, 3 * width :]], axis=1),
        )
        whole = in_order(core, kept, swap(sent, "core"))
        mine = whole[:, :width]
        other = swap(whole[:, width:].astype(BF16), "x").astype(values.dtype)
        return in_order(x, mine, other)

    layer_result_output = hand_back(layer_result.astype(BF16))

    grad_pair = pair_columns(cotangent)
    cotangent_here = spread(
        (pick(grad_pair, core, half), swap(pick(grad_pair, 1 - core, half), "core"))
    ).astype(F32)
    grad_resid_two, grad_gain_two, grad_shift_two = normalize_back(
        cotangent_here, second_standardized, second_inverse, gain_two
    )
    grad_down_bias = jnp.sum(grad_resid_two, axis=0)
    grad_down_all = gather_core(grad_resid_two.astype(BF16))

    def row_blocks(grad):
        amount = grad.shape[1] // 2
        sides = [
            [grad[r * width : (r + 1) * width, s * amount : (s + 1) * amount] for s in range(2)]
            for r in range(4)
        ]
        return [sides[0], sides[2]], [sides[1], sides[3]]

    def column_blocks(grad):
        amount = grad.shape[0] // 2
        sides = [
            [grad[s * amount : (s + 1) * amount, r * width : (r + 1) * width] for s in range(2)]
            for r in range(4)
        ]
        return [sides[0], sides[2]], [sides[1], sides[3]]

    def settle(grad, blocks, axis, after):
        first, second = over_groups(scatter_plane(*blocks(grad.astype(BF16))), after)
        mine, other = by_core(first, second)
        return in_order(core, mine, swap(other, "core"), axis).astype(F32), (first, second)

    across = ((0,), (0,))
    turned = ((1,), (1,))
    grad_down_weight, done = settle(
        dot(hidden, grad_down_all, across), column_blocks, 0, None
    )
    (grad_upward,) = gelu_pull(dot(grad_down_all, down_full, turned))
    grad_upward = grad_upward.astype(BF16)
    grad_up_bias = jnp.sum(grad_upward, axis=0, dtype=F32)
    grad_up_weight, done = settle(dot(normed_all, grad_upward, across), row_blocks, 1, done)
    grad_normalized = grad_resid_two + reduce_core(dot(grad_upward, up_full, turned))
    grad_resid_one, grad_gain_one, grad_shift_one = normalize_back(
        grad_normalized, first_standardized, first_inverse, gain_one
    )
    grad_out_bias = jnp.sum(grad_resid_one, axis=0)
    grad_attn_all = gather_core(grad_resid_one.astype(BF16))
    grad_out_weight, done = settle(
        dot(context, grad_attn_all, across), column_blocks, 0, done
    )
    grad_context = dot(grad_attn_all, out_full, turned).astype(BF16)
    grad_mixed = attend_back(mixed, grad_context, log_sums, place)
    grad_qkv_weight, done = settle(dot(tokens_all, grad_mixed, across), row_blocks, 1, done)
    grad_tokens = hand_back(grad_resid_one + reduce_core(dot(grad_mixed, qkv_full, turned)))

    def row_wide(values):
        blocks = values.reshape(2, 2, width)
        return turn(blocks, x, 0).reshape(-1)

    def col_wide(values):
        blocks = values.reshape(2, 1, -1)
        blocks = turn(blocks, col, 0)
        zeros = jnp.zeros_like(blocks)
        return in_order(core, blocks, zeros, 1).reshape(-1)

    everywhere = ("dp", "x", "core", "col")
    row_list = [
        grad_out_bias,
        grad_gain_one,
        grad_shift_one,
        grad_down_bias,
        grad_gain_two,
        grad_shift_two,
    ]
    early = lax.psum(
        jnp.concatenate([row_wide(values) for values in row_list] + [col_wide(grad_up_bias)]),
        everywhere,
    )
    row_sums = [
        lax.dynamic_slice_in_dim(
            early, index * 4 * width + (2 * x + core) * width, width, 0
        )
        for index in range(count)
    ]
    up_sum = lax.dynamic_slice_in_dim(early, count * 4 * width + col * up_amount, up_amount, 0)
    head_sums = jnp.sum(grad_mixed, axis=0, dtype=F32).reshape(-1, 3, HD)
    late = lax.psum(
        jnp.stack([col_wide(head_sums[:, 0].reshape(-1)), col_wide(head_sums[:, 2].reshape(-1))]),
        everywhere,
    )
    late = lax.dynamic_slice_in_dim(late, col * head_amount, head_amount, 1)
    return (
        layer_result_output,
        grad_tokens,
        grad_qkv_weight,
        late[0],
        late[1],
        grad_out_weight,
        row_sums[0],
        row_sums[1],
        row_sums[2],
        grad_up_weight,
        up_sum,
        grad_down_weight,
        row_sums[3],
        row_sums[4],
        row_sums[5],
    )


def solution(mesh):
    sizes = mesh.shape
    fine = Mesh(
        mesh.devices.reshape(sizes["dp"], sizes["row"] // 2, 2, sizes["col"]),
        ("dp", "x", "core", "col"),
    )
    row = ("x", "core")
    activation = P(("dp", "col"), row)
    return jax.shard_map(
        shards,
        mesh=fine,
        in_specs=(
            activation,
            P("dp"),
            P(row, "col"),
            P("col"),
            P("col"),
            P("col", row),
            P(row),
            P(row),
            P(row),
            P(row, "col"),
            P("col"),
            P("col", row),
            P(row),
            P(row),
            P(row),
            activation,
        ),
        out_specs=(
            activation,
            activation,
            P(row, "col"),
            P("col"),
            P("col"),
            P("col", row),
            P(row),
            P(row),
            P(row),
            P(row, "col"),
            P("col"),
            P("col", row),
            P(row),
            P(row),
            P(row),
        ),
        check_vma=False,
    )
```

time: 2040 us -> 645 us (0.32)
  waiting for transfers between devices: 1540 us -> 228 us
  matrix products: 200 us -> 106 us
  Pallas kernels: 0 us -> 58.7 us
  starting transfers between devices: 1.69 us -> 57.7 us
  blocking collectives: 98 us -> 56.8 us
  other arithmetic: 102 us -> 67.3 us
  local copies, waits for them, and re-layouts: 75.9 us -> 43.9 us
    reduce_scatter x8 -> x0, waiting for transfers between devices: 937 us -> none  [the longest x4 721 us: row_product(): lax.psum_scatter(lax.dot_general(gathered, weight, numbers, preferred_ele...]
    all_gather x8 -> x0, waiting for transfers between devices: 437 us -> none  [the longest x2 162 us: input_fold(): shard_piece = lax.all_gather(grad_local, 'row', axis=0, tiled=True)]
    ppermute x0 -> x71, waiting for transfers between devices: none -> 125 us  [swap(): return lax.ppermute(values, axis, [(0, 1), (1, 0)])]
    dot_general x26 -> x12, matrix products: 200 us -> 106 us  [dot(): lax.dot_general(left, right, (contract, ((), ())), preferred_element_type...]
    pallas_call x0 -> x2, Pallas kernels: none -> 58.7 us  [the longest x1 29.4 us: attend_back(): pl.pallas_call(attend_back_body, grid=(pairs,), in_specs=[pl.BlockSpec(me...]
    ppermute x0 -> x71, starting transfers between devices: none -> 57.5 us  [swap(): return lax.ppermute(values, axis, [(0, 1), (1, 0)])]
    psum x1 -> x4, waiting for transfers between devices: 160 us -> 103 us  [over_groups(): return lax.psum(values, 'dp')]
    psum x8 -> x1, blocking collectives: 98 us -> 47.2 us  [shards(): lax.psum(jnp.stack([col_wide(head_sums[:, 0].reshape(-1)), col_wide(head_...]
  transfers between devices with their start and end apart: 17 -> 75, of which waited for: 17 -> 25; matrix products, arithmetic and copies ran while one was open for 2% -> 28% of each run, Pallas kernels for 0% -> 9%
where the time goes in v1:
time: 645 us; the launch traced here: 635 us
  waiting for transfers between devices  228 us (35%)
  matrix products  106 us (16%)
  other arithmetic  67.3 us (10%)
  Pallas kernels  58.7 us (9%)
  starting transfers between devices  57.7 us (9%)
  blocking collectives  56.8 us (9%)
  local copies, waits for them, and re-layouts  43.9 us (7%)
  between operations  16 us (2%)
    ppermute x71, waiting for transfers between devices, swap(): return lax.ppermute(values, axis, [(0, 1), (1, 0)])  125 us
    dot_general x12, matrix products, dot(): lax.dot_general(left, right, (contract, ((), ())), preferred_element_type...  106 us
    psum x4, waiting for transfers between devices, over_groups(): return lax.psum(values, 'dp')  103 us
    ppermute x71, starting transfers between devices, swap(): return lax.ppermute(values, axis, [(0, 1), (1, 0)])  57.5 us
    psum x1, blocking collectives, shards(): lax.psum(jnp.stack([col_wide(head_sums[:, 0].reshape(-1)), col_wide(head_...  47.2 us
    pallas_call x1, Pallas kernels, attend_back(): pl.pallas_call(attend_back_body, grid=(pairs,), in_specs=[pl.BlockSpec(me...  29.4 us
    pallas_call x1, Pallas kernels, attend(): pl.pallas_call(attend_body, grid=(pairs,), in_specs=[pl.BlockSpec(memory_...  29.3 us
    unnamed x217, local copies, waits for them, and re-layouts  18.7 us
  transfers between devices with their start and end apart: 75, of which 25 were waited for; matrix products, arithmetic and copies ran while one was open for 28% of the time, Pallas kernels for 9%

profile of v1, /device:TPU:0, one launch (start us, length us, event | category | flops | bytes accessed | tf_op | source)
XLA Modules:
  0.0 635.3 jit_solution(12033976643709378888)
XLA Ops:
  33.0 5.7 collective-permute-done.5
  43.6 15.6 %collective-permute-done.13 = bf16[256,256]{1,0:T(8,128)(2,1)S(1)} collective-permute-done((bf16[256,256]{1,0:T(8,128)(2,1)S(1)}, bf16[256,256]{1,0:T(8,128)(2,1)S(1)}, u32[]{:S(2)}, u32[]{:S(2)}) %collective-permute-start.13) | collective-permute-done | bytes 131104 | tf_op jit(solution)/shard_map/ppermute | solution.py:19
  68.4 29.3 %attend.1 = (bf16[1024,512]{1,0:T(8,128)(2,1)S(1)}, f32[4,2,1024]{2,1,0:T(2,128)S(1)}) custom-call(s32[2]{0:T(128)S(1)} %pad_add_fusion.place_ref, bf16[1024,1536]{1,0:T(8,128)(2,1)S(1)} %add_convert_fusion.1.mixed_ref), custom_call_target="tpu_custom_call" | custom-call | flops 2147483648 | bytes 4718592 | tf_op jit(solution)/shard_map/attend/pallas_call | solution.py:105
  105.6 5.2 all-gather.2
  121.6 5.5 collective-permute-done.21
  127.6 10.4 %collective-permute-done.20 = bf16[256,1024]{1,0:T(8,128)(2,1)S(1)} collective-permute-done((bf16[256,1024]{1,0:T(8,128)(2,1)S(1)}, bf16[256,1024]{1,0:T(8,128)(2,1)S(1)}, u32[]{:S(2)}, u32[]{:S(2)}) %collective-permute-start.20) | collective-permute-done | bytes 524320 | tf_op jit(solution)/shard_map/ppermute | solution.py:19
  141.6 8.0 %collective-permute-done.26 = bf16[1024,256]{1,0:T(8,128)(2,1)S(1)} collective-permute-done((bf16[1024,256]{1,0:T(8,128)(2,1)S(1)}, bf16[1024,256]{1,0:T(8,128)(2,1)S(1)}, u32[]{:S(2)}, u32[]{:S(2)}) %collective-permute-start.26) | collective-permute-done | bytes 524320 | tf_op jit(solution)/shard_map/ppermute | solution.py:19
  154.4 9.6 %collective-permute-done.22 = bf16[256,1024]{1,0:T(8,128)(2,1)S(1)} collective-permute-done((bf16[256,1024]{1,0:T(8,128)(2,1)S(1)}, bf16[256,1024]{1,0:T(8,128)(2,1)S(1)}, u32[]{:S(2)}, u32[]{:S(2)}) %collective-permute-start.22) | collective-permute-done | bytes 524320 | tf_op jit(solution)/shard_map/ppermute | solution.py:19
  167.2 40.5 %multiply_convert_fusion = (bf16[1024,2048]{1,0:T(8,128)(2,1)}, f32[1024,2048]{1,0:T(8,128)}, f32[1024,2048]{1,0:T(8,128)}) fusion(f32[2048]{0:T(1024)S(1)} %bitcast.76, bf16[256,1024]{1,0:T(8,128)(2,1)S(1)} %collective-permute-done.24, bf16[256,1024]{1,0:T(8,128)(2,1)S(1)} %collective-permute-done.23, bf16[256,1024]{1,0:T(8,128)(2,1)S(1)} %collective-permute-done.22, ...), kind=kOutput, calls=%fused_computation.4 | convolution fusion | flops 4471128064 | bytes 27271168 | tf_op jit(solution)/shard_map/dot_general | solution.py:35
  207.8 7.6 %fusion.51 = f32[1024,1024]{0,1:T(8,128)S(1)} fusion(bf16[1024,2048]{1,0:T(8,128)(2,1)} %get-tuple-element.117, bf16[1024,256]{1,0:T(8,128)(2,1)S(1)} %collective-permute-done.31, bf16[1024,256]{1,0:T(8,128)(2,1)S(1)} %collective-permute-done.30, bf16[1024,256]{1,0:T(8,128)(2,1)S(1)} %collective-permute-done.29, ...), kind=kOutput, calls=%fused_computation.205 | convolution fusion | flops 4328521728 | bytes 12582912 | tf_op jit(solution)/shard_map/dot_general | solution.py:35
  222.8 12.8 %collective-permute-done.35 = bf16[1024,256]{0,1:T(8,128)(2,1)S(1)} collective-permute-done((bf16[1024,256]{0,1:T(8,128)(2,1)}, bf16[1024,256]{0,1:T(8,128)(2,1)S(1)}, u32[]{:S(2)}, u32[]{:S(2)}) %collective-permute-start.35) | collective-permute-done | bytes 524320 | tf_op jit(solution)/shard_map/ppermute | solution.py:19
  251.3 6.5 %convolution_convert_fusion.1 = bf16[2048,1024]{1,0:T(8,128)(2,1)S(1)} fusion(bf16[1024,2048]{1,0:T(8,128)(2,1)S(1)} %copy-done.96, bf16[512,1024]{0,1:T(8,128)(2,1)} %collective-permute-done.37, bf16[512,1024]{0,1:T(8,128)(2,1)} %get-tuple-element.133), kind=kOutput, calls=%fused_computation.23 | convolution fusion | flops 4301258752 | bytes 10485760 | tf_op jit(solution)/shard_map/dot_general | solution.py:35
  263.7 16.7 %convert_reduce_fusion = (f32[2048]{0:T(1024)S(1)}, bf16[1024,2048]{1,0:T(8,128)(2,1)}) fusion(f32[1024,2048]{1,0:T(8,128)} %get-tuple-element.118, bf16[1024,256]{1,0:T(8,128)(2,1)} %copy-done.78, bf16[1024,256]{1,0:T(8,128)(2,1)} %copy-done.77, bf16[1024,256]{1,0:T(8,128)(2,1)} %copy-done.74, bf16[1024,256]{1,0:T(8,128)(2,1)} %copy-done.76, ...), kind=kOutput, calls=%fused_computation.2 | convolution fusion | flops 4368365568 | bytes 27279360 | tf_op jit(solution)/shard_map/dot_general | solution.py:35
  280.5 7.5 %convolution_convert_fusion.2 = bf16[1024,2048]{1,0:T(8,128)(2,1)S(1)} fusion(bf16[1024,2048]{1,0:T(8,128)(2,1)} %get-tuple-element.215, bf16[512,1024]{0,1:T(8,128)(2,1)} %copy-done.58, bf16[512,1024]{0,1:T(8,128)(2,1)} %copy-done.30), kind=kOutput, calls=%fused_computation.24 | convolution fusion | flops 4301258752 | bytes 10485760 | tf_op jit(solution)/shard_map/dot_general | solution.py:35
  305.1 12.0 %collective-permute-done.66 = bf16[1024,256]{1,0:T(8,128)(2,1)S(1)} collective-permute-done((bf16[1024,256]{1,0:T(8,128)(2,1)S(1)}, bf16[1024,256]{1,0:T(8,128)(2,1)S(1)}, u32[]{:S(2)}, u32[]{:S(2)}) %collective-permute-start.66) | collective-permute-done | bytes 524320 | tf_op jit(solution)/shard_map/ppermute | solution.py:19
  322.6 5.8 collective-permute-done.60
  359.7 38.7 %all-reduce.22.cloned.1.call-done = (bf16[1024,256]{1,0:T(8,128)(2,1)}, bf16[1024,256]{1,0:T(8,128)(2,1)}) async-done(((bf16[1024,256]{1,0:T(8,128)(2,1)}, bf16[1024,256]{1,0:T(8,128)(2,1)}), (bf16[1024,256]{1,0:T(8,128)(2,1)}, bf16[1024,256]{1,0:T(8,128)(2,1)})) %all-reduce.22.cloned.1.call-update) | async-done | bytes 1048592 | tf_op jit(solution)/shard_map/psum | solution.py:65
  403.0 29.4 %attend_back.1 = bf16[1024,1536]{1,0:T(8,128)(2,1)S(1)} custom-call(s32[2]{0:T(128)S(1)} %copy-done.1, bf16[1024,1536]{1,0:T(8,128)(2,1)S(1)} %copy-done.5, bf16[1024,512]{1,0:T(8,128)(2,1)S(1)} %convolution_convert_fusion.4.grad_ref, f32[4,2,1024]{2,1,0:T(2,128)S(1)} %get-tuple-element.24.sums_ref), custom_call_target="tpu_custom_call" | custom-call | flops 5368709120 | bytes 7864320 | tf_op jit(solution)/shard_map/attend_back/pallas_call | solution.py:164
  433.0 6.7 %convolution_convert_fusion = bf16[1024,1536]{1,0:T(8,128)(2,1)} fusion(bf16[1024,1536]{1,0:T(8,128)(2,1)S(1)} %attend_back.1, bf16[1024,256]{0,1:T(8,128)(2,1)S(1)} %copy-done.23, bf16[1024,256]{0,1:T(8,128)(2,1)S(1)} %copy-done.19, bf16[1024,256]{0,1:T(8,128)(2,1)S(1)} %copy-done.21, bf16[1024,256]{0,1:T(8,128)(2,1)S(1)} %copy-done.17), kind=kOutput, calls=%fused_computation.22 | convolution fusion | flops 3231186944 | bytes 8388608 | tf_op jit(solution)/shard_map/dot_general | solution.py:35
  450.5 7.5 %fusion.50 = f32[1024,1024]{0,1:T(8,128)S(1)} fusion(bf16[1024,1536]{1,0:T(8,128)(2,1)S(1)} %attend_back.1, bf16[256,768]{1,0:T(8,128)(2,1)} %copy-done.82, bf16[256,768]{1,0:T(8,128)(2,1)} %copy-done.80, bf16[256,768]{1,0:T(8,128)(2,1)} %copy-done.81, bf16[256,768]{1,0:T(8,128)(2,1)} %collective-permute-done.5, ...), kind=kOutput, calls=%fused_computation.204 | convolution fusion | flops 3246391296 | bytes 10485760 | tf_op jit(solution)/shard_map/dot_general | solution.py:35
  467.3 47.2 %all-reduce.6 = (f32[2,1024]{1,0:T(2,128)S(1)}, f32[10240]{0:T(1024)S(1)}) all-reduce(f32[2,1024]{1,0:T(2,128)S(1)} %pad_maximum_fusion.23, f32[10240]{0:T(1024)S(1)} %constant_dynamic-update-slice_fusion), channel_id=1, replica_groups=mesh['dp'=4,'x'=2,'core'=2,'col'=2] {'dp','x','core','col'}, use_global_device_ids=true, to_apply=%region_17.18 | all-reduce | flops 12288 | bytes 98304 | tf_op jit(solution)/shard_map/psum | solution.py:456
  534.8 27.1 %all-reduce.18.cloned.1.call-done = (bf16[256,256]{1,0:T(8,128)(2,1)}, bf16[256,256]{1,0:T(8,128)(2,1)}) async-done(((bf16[256,256]{1,0:T(8,128)(2,1)}, bf16[256,256]{1,0:T(8,128)(2,1)}), (bf16[256,256]{1,0:T(8,128)(2,1)}, bf16[256,256]{1,0:T(8,128)(2,1)})) %all-reduce.18.cloned.1.call-update) | async-done | bytes 262160 | tf_op jit(solution)/shard_map/psum | solution.py:65
  571.1 37.6 %all-reduce.16.cloned.1.call-done = (bf16[256,768]{1,0:T(8,128)(2,1)}, bf16[256,768]{1,0:T(8,128)(2,1)}) async-done(((bf16[256,768]{1,0:T(8,128)(2,1)}, bf16[256,768]{1,0:T(8,128)(2,1)}), (bf16[256,768]{1,0:T(8,128)(2,1)}, bf16[256,768]{1,0:T(8,128)(2,1)})) %all-reduce.16.cloned.1.call-update) | async-done | bytes 786448 | tf_op jit(solution)/shard_map/psum | solution.py:65
  617.9 8.5 %collective-permute-done.42 = bf16[1024,256]{0,1:T(8,128)(2,1)S(1)} collective-permute-done((bf16[1024,256]{0,1:T(8,128)(2,1)S(1)}, bf16[1024,256]{0,1:T(8,128)(2,1)S(1)}, u32[]{:S(2)}, u32[]{:S(2)}) %collective-permute-start.42) | collective-permute-done | bytes 524320 | tf_op jit(solution)/shard_map/ppermute | solution.py:19
  (487 shorter events, 217.9 us)
Async XLA Ops:
  7.2 391.2 %all-reduce.22.cloned.1.call-start = ((), (), s32[]{:S(2)}) async-start(), calls=%async_computation.3 | async-start | bytes 2097152 | tf_op jit(solution)/shard_map/psum | solution.py:65
  59.3 38.5 %collective-permute-start.11 = (bf16[256,256]{1,0:T(8,128)(2,1)S(1)}, bf16[256,256]{1,0:T(8,128)(2,1)S(1)}, u32[]{:S(2)}, u32[]{:S(2)}) collective-permute-start(bf16[256,256]{1,0:T(8,128)(2,1)S(1)} %get-tuple-element.194), channel_id=1, source_target_pairs={{0,4},{4,0},{1,5},{5,1},{2,6},{6,2},{3,7},{7,3},{8,12},{12,8},{9,1... | collective-permute-start | bytes 393224 | tf_op jit(solution)/shard_map/ppermute | solution.py:19
  59.6 38.2 %collective-permute-start.12 = (bf16[256,256]{1,0:T(8,128)(2,1)S(1)}, bf16[256,256]{1,0:T(8,128)(2,1)S(1)}, u32[]{:S(2)}, u32[]{:S(2)}) collective-permute-start(bf16[256,256]{1,0:T(8,128)(2,1)S(1)} %get-tuple-element.193), channel_id=1, source_target_pairs={{0,1},{1,0},{2,3},{3,2},{4,5},{5,4},{6,7},{7,6},{8,9},{9,8},{10,11... | collective-permute-start | bytes 393224 | tf_op jit(solution)/shard_map/ppermute | solution.py:19
  119.8 47.3 %collective-permute-start.17 = (bf16[512,1024]{0,1:T(8,128)(2,1)S(1)}, bf16[512,1024]{0,1:T(8,128)(2,1)S(1)}, u32[]{:S(2)}, u32[]{:S(2)}) collective-permute-start(bf16[512,1024]{0,1:T(8,128)(2,1)S(1)} %fusion.19), channel_id=1, source_target_pairs={{0,2},{2,0},{1,3},{3,1},{4,6},{6,4},{5,7},{7,5},{8,10},{10,8},{9,1... | collective-permute-start | bytes 3145736 | tf_op jit(solution)/shard_map/ppermute | solution.py:19
  149.6 58.1 %collective-permute-start.27 = (bf16[1024,256]{1,0:T(8,128)(2,1)S(1)}, bf16[1024,256]{1,0:T(8,128)(2,1)S(1)}, u32[]{:S(2)}, u32[]{:S(2)}) collective-permute-start(bf16[1024,256]{1,0:T(8,128)(2,1)S(1)} %get-tuple-element.152), channel_id=1, source_target_pairs={{0,4},{4,0},{1,5},{5,1},{2,6},{6,2},{3,7},{7,3},{8,12},{12,8},{9,1... | collective-permute-start | bytes 1572872 | tf_op jit(solution)/shard_map/ppermute | solution.py:19
  152.8 54.9 %collective-permute-start.28 = (bf16[1024,256]{1,0:T(8,128)(2,1)S(1)}, bf16[1024,256]{1,0:T(8,128)(2,1)S(1)}, u32[]{:S(2)}, u32[]{:S(2)}) collective-permute-start(bf16[1024,256]{1,0:T(8,128)(2,1)S(1)} %get-tuple-element.151), channel_id=1, source_target_pairs={{0,1},{1,0},{2,3},{3,2},{4,5},{5,4},{6,7},{7,6},{8,9},{9,8},{10,11... | collective-permute-start | bytes 1572872 | tf_op jit(solution)/shard_map/ppermute | solution.py:19
  164.1 43.7 %collective-permute-start.30 = (bf16[1024,256]{1,0:T(8,128)(2,1)S(1)}, bf16[1024,256]{1,0:T(8,128)(2,1)S(1)}, u32[]{:S(2)}, u32[]{:S(2)}) collective-permute-start(bf16[1024,256]{1,0:T(8,128)(2,1)S(1)} %collective-permute-done.26), channel_id=1, source_target_pairs={{0,1},{1,0},{2,3},{3,2},{4,5},{5,4},{6,7},{7,6},{8,9},{9,8},{10,11... | collective-permute-start | bytes 1572872 | tf_op jit(solution)/shard_map/ppermute | solution.py:19
  165.7 42.1 %collective-permute-start.31 = (bf16[1024,256]{1,0:T(8,128)(2,1)S(1)}, bf16[1024,256]{1,0:T(8,128)(2,1)S(1)}, u32[]{:S(2)}, u32[]{:S(2)}) collective-permute-start(bf16[1024,256]{1,0:T(8,128)(2,1)S(1)} %collective-permute-done.29), channel_id=1, source_target_pairs={{0,4},{4,0},{1,5},{5,1},{2,6},{6,2},{3,7},{7,3},{8,12},{12,8},{9,1... | collective-permute-start | bytes 1572872 | tf_op jit(solution)/shard_map/ppermute | solution.py:19
  261.2 36.7 %collective-permute-start.65 = (bf16[1024,256]{1,0:T(8,128)(2,1)}, bf16[1024,256]{1,0:T(8,128)(2,1)}, u32[]{:S(2)}, u32[]{:S(2)}) collective-permute-start(bf16[1024,256]{1,0:T(8,128)(2,1)} %get-tuple-element.124), channel_id=1, source_target_pairs={{0,4},{4,0},{1,5},{5,1},{2,6},{6,2},{3,7},{7,3},{8,12},{12,8},{9,1... | collective-permute-start | bytes 1572872 | tf_op jit(solution)/shard_map/ppermute | solution.py:19
  261.7 42.3 %collective-permute-start.62 = (bf16[1024,256]{1,0:T(8,128)(2,1)}, bf16[1024,256]{1,0:T(8,128)(2,1)}, u32[]{:S(2)}, u32[]{:S(2)}) collective-permute-start(bf16[1024,256]{1,0:T(8,128)(2,1)} %get-tuple-element.125), channel_id=1, source_target_pairs={{0,1},{1,0},{2,3},{3,2},{4,5},{5,4},{6,7},{7,6},{8,9},{9,8},{10,11... | collective-permute-start | bytes 1572872 | tf_op jit(solution)/shard_map/ppermute | solution.py:19
  262.2 42.4 %collective-permute-start.64 = (bf16[1024,256]{1,0:T(8,128)(2,1)}, bf16[1024,256]{1,0:T(8,128)(2,1)}, u32[]{:S(2)}, u32[]{:S(2)}) collective-permute-start(bf16[1024,256]{1,0:T(8,128)(2,1)} %get-tuple-element.123), channel_id=1, source_target_pairs={{0,4},{4,0},{1,5},{5,1},{2,6},{6,2},{3,7},{7,3},{8,12},{12,8},{9,1... | collective-permute-start | bytes 1572872 | tf_op jit(solution)/shard_map/ppermute | solution.py:19
  297.9 54.4 %collective-permute-start.38 = (f32[512,1024]{0,1:T(8,128)}, f32[512,1024]{0,1:T(8,128)}, u32[]{:S(2)}, u32[]{:S(2)}) collective-permute-start(f32[512,1024]{0,1:T(8,128)} %slice.341), channel_id=1, source_target_pairs={{0,2},{2,0},{1,3},{3,1},{4,6},{6,4},{5,7},{7,5},{8,10},{10,8},{9,1... | collective-permute-start | bytes 6291464 | tf_op jit(solution)/shard_map/ppermute | solution.py:19
  345.9 180.0 %all-reduce.20.cloned.1.call-start = ((), (), s32[]{:S(2)}) async-start(), calls=%async_computation.2 | async-start | bytes 2097152 | tf_op jit(solution)/shard_map/psum | solution.py:65
  359.4 41.3 %collective-permute-start.39 = (bf16[512,1024]{0,1:T(8,128)(2,1)S(1)}, bf16[512,1024]{0,1:T(8,128)(2,1)S(1)}, u32[]{:S(2)}, u32[]{:S(2)}) collective-permute-start(bf16[512,1024]{0,1:T(8,128)(2,1)S(1)} %convert_element_type.240), channel_id=1, source_target_pairs={{0,2},{2,0},{1,3},{3,1},{4,6},{6,4},{5,7},{7,5},{8,10},{10,8},{9,1... | collective-permute-start | bytes 3145736 | tf_op jit(solution)/shard_map/ppermute | solution.py:19
  398.4 163.4 %all-reduce.18.cloned.1.call-start = ((), (), s32[]{:S(2)}) async-start(), calls=%async_computation.1 | async-start | bytes 524288 | tf_op jit(solution)/shard_map/psum | solution.py:65
  459.5 102.4 %collective-permute-start.40 = (f32[512,1024]{0,1:T(8,128)}, f32[512,1024]{0,1:T(8,128)}, u32[]{:S(2)}, u32[]{:S(2)}) collective-permute-start(f32[512,1024]{0,1:T(8,128)} %slice.343), channel_id=1, source_target_pairs={{0,2},{2,0},{1,3},{3,1},{4,6},{6,4},{5,7},{7,5},{8,10},{10,8},{9,1... | collective-permute-start | bytes 6291464 | tf_op jit(solution)/shard_map/ppermute | solution.py:19
  460.6 57.9 %collective-permute-start.44 = (bf16[256,768]{1,0:T(8,128)(2,1)}, bf16[256,768]{1,0:T(8,128)(2,1)}, u32[]{:S(2)}, u32[]{:S(2)}) collective-permute-start(bf16[256,768]{1,0:T(8,128)(2,1)} %get-tuple-element.138), channel_id=1, source_target_pairs={{0,1},{1,0},{2,3},{3,2},{4,5},{5,4},{6,7},{7,6},{8,9},{9,8},{10,11... | collective-permute-start | bytes 1179656 | tf_op jit(solution)/shard_map/ppermute | solution.py:19
  462.8 55.7 %collective-permute-start.46 = (bf16[256,768]{1,0:T(8,128)(2,1)}, bf16[256,768]{1,0:T(8,128)(2,1)}, u32[]{:S(2)}, u32[]{:S(2)}) collective-permute-start(bf16[256,768]{1,0:T(8,128)(2,1)} %get-tuple-element.136), channel_id=1, source_target_pairs={{0,4},{4,0},{1,5},{5,1},{2,6},{6,2},{3,7},{7,3},{8,12},{12,8},{9,1... | collective-permute-start | bytes 1179656 | tf_op jit(solution)/shard_map/ppermute | solution.py:19
  465.2 49.3 %collective-permute-start.54 = (bf16[256,256]{1,0:T(8,128)(2,1)}, bf16[256,256]{1,0:T(8,128)(2,1)}, u32[]{:S(2)}, u32[]{:S(2)}) collective-permute-start(bf16[256,256]{1,0:T(8,128)(2,1)} %add_convert_fusion.16), channel_id=1, source_target_pairs={{0,1},{1,0},{2,3},{3,2},{4,5},{5,4},{6,7},{7,6},{8,9},{9,8},{10,11... | collective-permute-start | bytes 393224 | tf_op jit(solution)/shard_map/ppermute | solution.py:19
  466.6 53.9 %collective-permute-start.48 = (bf16[256,768]{1,0:T(8,128)(2,1)}, bf16[256,768]{1,0:T(8,128)(2,1)}, u32[]{:S(2)}, u32[]{:S(2)}) collective-permute-start(bf16[256,768]{1,0:T(8,128)(2,1)} %add_convert_fusion.12), channel_id=1, source_target_pairs={{0,1},{1,0},{2,3},{3,2},{4,5},{5,4},{6,7},{7,6},{8,9},{9,8},{10,11... | collective-permute-start | bytes 1179656 | tf_op jit(solution)/shard_map/ppermute | solution.py:19
  525.1 40.3 %collective-permute-start.70 = (bf16[1024,256]{1,0:T(8,128)(2,1)}, bf16[1024,256]{1,0:T(8,128)(2,1)}, u32[]{:S(2)}, u32[]{:S(2)}) collective-permute-start(bf16[1024,256]{1,0:T(8,128)(2,1)} %get-tuple-element.158), channel_id=1, source_target_pairs={{0,2},{2,0},{1,3},{3,1},{4,6},{6,4},{5,7},{7,5},{8,10},{10,8},{9,1... | collective-permute-start | bytes 1572872 | tf_op jit(solution)/shard_map/ppermute | solution.py:19
  525.9 82.7 %all-reduce.16.cloned.1.call-start = ((), (), s32[]{:S(2)}) async-start(), calls=%async_computation | async-start | bytes 1572864 | tf_op jit(solution)/shard_map/psum | solution.py:65
  565.3 44.6 %collective-permute-start.41 = (f32[512,512]{0,1:T(8,128)S(1)}, f32[512,512]{0,1:T(8,128)}, u32[]{:S(2)}, u32[]{:S(2)}) collective-permute-start(f32[512,512]{0,1:T(8,128)S(1)} %get-tuple-element.142), channel_id=1, source_target_pairs={{0,2},{2,0},{1,3},{3,1},{4,6},{6,4},{5,7},{7,5},{8,10},{10,8},{9,1... | collective-permute-start | bytes 3145736 | tf_op jit(solution)/shard_map/ppermute | solution.py:19
  569.0 44.5 %collective-permute-start.69 = (bf16[256,1024]{1,0:T(8,128)(2,1)S(1)}, bf16[256,1024]{1,0:T(8,128)(2,1)}, u32[]{:S(2)}, u32[]{:S(2)}) collective-permute-start(bf16[256,1024]{1,0:T(8,128)(2,1)S(1)} %get-tuple-element.160), channel_id=1, source_target_pairs={{0,2},{2,0},{1,3},{3,1},{4,6},{6,4},{5,7},{7,5},{8,10},{10,8},{9,1... | collective-permute-start | bytes 1572872 | tf_op jit(solution)/shard_map/ppermute | solution.py:19
  (149 other events, 3258.5 us)
Sparse Core Ops, SparseCore 0:
  346.0 52.3 all-reduce.21
  401.5 51.5 all-reduce.19
  526.0 35.7 all-reduce.17
  564.8 43.7 all-reduce.15

commit v2 on v1

--- a/solution.py
+++ b/solution.py
@@ -347,10 +347,9 @@
     )
     normed_all = gather_core(first_normalized.astype(BF16))
     upward = dot(normed_all, up_full) + up_bias_here
-    hidden_f, gelu_pull = jax.vjp(
-        lambda values: jax.nn.gelu(values, approximate=False), upward
-    )
-    hidden = hidden_f.astype(BF16)
+    portion = 0.5 * (1.0 + lax.erf(upward * (0.5**0.5)))
+    slope = portion + upward * (jnp.exp(-0.5 * upward * upward) * (0.5 / jnp.pi) ** 0.5)
+    hidden = (upward * portion).astype(BF16)
     second_residual = first_normalized + reduce_core(dot(hidden, down_full)) + down_bias_all
     layer_result, second_standardized, second_inverse = normalize(
         second_residual, gain_two, shift_two
@@ -394,32 +393,30 @@
         ]
         return [sides[0], sides[2]], [sides[1], sides[3]]
 
-    def settle(grad, blocks, axis, after):
-        first, second = over_groups(scatter_plane(*blocks(grad.astype(BF16))), after)
+    def plane_sums(grad, blocks):
+        return scatter_plane(*blocks(grad.astype(BF16)))
+
+    def settle(first, second, axis):
         mine, other = by_core(first, second)
-        return in_order(core, mine, swap(other, "core"), axis).astype(F32), (first, second)
+        return in_order(core, mine, swap(other, "core"), axis).astype(F32)
 
     across = ((0,), (0,))
     turned = ((1,), (1,))
-    grad_down_weight, done = settle(
-        dot(hidden, grad_down_all, across), column_blocks, 0, None
-    )
-    (grad_upward,) = gelu_pull(dot(grad_down_all, down_full, turned))
-    grad_upward = grad_upward.astype(BF16)
+    down_sums = plane_sums(dot(hidden, grad_down_all, across), column_blocks)
+    grad_upward = (dot(grad_down_all, down_full, turned) * slope).astype(BF16)
     grad_up_bias = jnp.sum(grad_upward, axis=0, dtype=F32)
-    grad_up_weight, done = settle(dot(normed_all, grad_upward, across), row_blocks, 1, done)
+    up_sums = plane_sums(dot(normed_all, grad_upward, across), row_blocks)
+    ahead = over_groups(down_sums + up_sums, None)
     grad_normalized = grad_resid_two + reduce_core(dot(grad_upward, up_full, turned))
     grad_resid_one, grad_gain_one, grad_shift_one = normalize_back(
         grad_normalized, first_standardized, first_inverse, gain_one
     )
     grad_out_bias = jnp.sum(grad_resid_one, axis=0)
     grad_attn_all = gather_core(grad_resid_one.astype(BF16))
-    grad_out_weight, done = settle(
-        dot(context, grad_attn_all, across), column_blocks, 0, done
-    )
+    out_sums = plane_sums(dot(context, grad_attn_all, across), column_blocks)
     grad_context = dot(grad_attn_all, out_full, turned).astype(BF16)
     grad_mixed = attend_back(mixed, grad_context, log_sums, place)
-    grad_qkv_weight, done = settle(dot(tokens_all, grad_mixed, across), row_blocks, 1, done)
+    qkv_sums = plane_sums(dot(tokens_all, grad_mixed, across), row_blocks)
     grad_tokens = hand_back(grad_resid_one + reduce_core(dot(grad_mixed, qkv_full, turned)))
 
     def row_wide(values):
@@ -432,7 +429,6 @@
         zeros = jnp.zeros_like(blocks)
         return in_order(core, blocks, zeros, 1).reshape(-1)
 
-    everywhere = ("dp", "x", "core", "col")
     row_list = [
         grad_out_bias,
         grad_gain_one,
@@ -441,10 +437,28 @@
         grad_gain_two,
         grad_shift_two,
     ]
-    early = lax.psum(
-        jnp.concatenate([row_wide(values) for values in row_list] + [col_wide(grad_up_bias)]),
-        everywhere,
-    )
+    head_sums = jnp.sum(grad_mixed, axis=0, dtype=F32).reshape(-1, 3, HD)
+
+    def plane_total(parts):
+        total = jnp.concatenate(parts)
+        for axis in ("core", "x", "col"):
+            total = total + swap(total, axis)
+        return total
+
+    early = plane_total([row_wide(values) for values in row_list] + [col_wide(grad_up_bias)])
+    late = plane_total(
+        [col_wide(head_sums[:, 0].reshape(-1)), col_wide(head_sums[:, 2].reshape(-1))]
+    )
+    down_first, down_second, up_first, up_second = ahead
+    out_first, out_second, qkv_first, qkv_second, early, late = over_groups(
+        out_sums + qkv_sums + (early, late), ahead
+    )
+    early = early.astype(F32)
+    late = late.astype(F32).reshape(2, -1)
+    grad_down_weight = settle(down_first, down_second, 0)
+    grad_up_weight = settle(up_first, up_second, 1)
+    grad_out_weight = settle(out_first, out_second, 0)
+    grad_qkv_weight = settle(qkv_first, qkv_second, 1)
     row_sums = [
         lax.dynamic_slice_in_dim(
             early, index * 4 * width + (2 * x + core) * width, width, 0
@@ -452,11 +466,6 @@
         for index in range(count)
     ]
     up_sum = lax.dynamic_slice_in_dim(early, count * 4 * width + col * up_amount, up_amount, 0)
-    head_sums = jnp.sum(grad_mixed, axis=0, dtype=F32).reshape(-1, 3, HD)
-    late = lax.psum(
-        jnp.stack([col_wide(head_sums[:, 0].reshape(-1)), col_wide(head_sums[:, 2].reshape(-1))]),
-        everywhere,
-    )
     late = lax.dynamic_slice_in_dim(late, col * head_amount, head_amount, 1)
     return (
         layer_result_output,

time: 645 us -> 545 us (0.84)
  waiting for transfers between devices: 228 us -> 178 us
  blocking collectives: 56.8 us -> 29.9 us
  matrix products: 106 us -> 84.6 us
    psum x4 -> x2, waiting for transfers between devices: 103 us -> 24.7 us  [over_groups(): return lax.psum(values, 'dp')]
    ppermute x71 -> x77, waiting for transfers between devices: 125 us -> 153 us  [swap(): return lax.ppermute(values, axis, [(0, 1), (1, 0)])]
    psum x1, blocking collectives: 47.2 us -> 20.2 us  [over_groups(): return lax.psum(values, 'dp')]
    dot_general x12, matrix products: 106 us -> 84.6 us  [dot(): lax.dot_general(left, right, (contract, ((), ())), preferred_element_type...]
    convert_element_type x8 -> x10, other arithmetic: 16.2 us -> 18.4 us  [over_groups(): values = tuple((value.astype(BF16) for value in values))]
    unnamed x217 -> x242, local copies, waits for them, and re-layouts: 18.7 us -> 20.3 us
    ppermute x71 -> x77, starting transfers between devices: 57.5 us -> 57.9 us  [swap(): return lax.ppermute(values, axis, [(0, 1), (1, 0)])]
  transfers between devices with their start and end apart: 75 -> 79, of which waited for: 25 -> 29; matrix products, arithmetic and copies ran while one was open for 28% -> 25% of each run, Pallas kernels for 9% -> 11%
where the time goes in v2:
time: 545 us; the launch traced here: 535 us
  waiting for transfers between devices  178 us (33%)
  matrix products  84.6 us (16%)
  other arithmetic  68.3 us (13%)
  Pallas kernels  58.3 us (11%)
  starting transfers between devices  57.9 us (11%)
  local copies, waits for them, and re-layouts  41.9 us (8%)
  blocking collectives  29.9 us (5%)
  between operations  16.3 us (3%)
    ppermute x77, waiting for transfers between devices, swap(): return lax.ppermute(values, axis, [(0, 1), (1, 0)])  153 us
    dot_general x12, matrix products, dot(): lax.dot_general(left, right, (contract, ((), ())), preferred_element_type...  84.6 us
    ppermute x77, starting transfers between devices, swap(): return lax.ppermute(values, axis, [(0, 1), (1, 0)])  57.9 us
    pallas_call x1, Pallas kernels, attend(): pl.pallas_call(attend_body, grid=(pairs,), in_specs=[pl.BlockSpec(memory_...  29.2 us
    pallas_call x1, Pallas kernels, attend_back(): pl.pallas_call(attend_back_body, grid=(pairs,), in_specs=[pl.BlockSpec(me...  29.1 us
    psum x2, waiting for transfers between devices, over_groups(): return lax.psum(values, 'dp')  24.7 us
    unnamed x242, local copies, waits for them, and re-layouts  20.3 us
    psum x1, blocking collectives, over_groups(): return lax.psum(values, 'dp')  20.2 us
  transfers between devices with their start and end apart: 79, of which 29 were waited for; matrix products, arithmetic and copies ran while one was open for 25% of the time, Pallas kernels for 11%

profile of v2, /device:TPU:0, one launch (start us, length us, event | category | flops | bytes accessed | tf_op | source)
XLA Modules:
  0.0 535.0 jit_solution(7860945328364186651)
XLA Ops:
  18.4 5.3 collective-permute-done
  43.6 15.6 %collective-permute-done.13 = bf16[256,256]{1,0:T(8,128)(2,1)S(1)} collective-permute-done((bf16[256,256]{1,0:T(8,128)(2,1)S(1)}, bf16[256,256]{1,0:T(8,128)(2,1)S(1)}, u32[]{:S(2)}, u32[]{:S(2)}) %collective-permute-start.13) | collective-permute-done | bytes 131104 | tf_op jit(solution)/shard_map/ppermute | solution.py:19
  68.9 29.2 %attend.1 = (bf16[1024,512]{1,0:T(8,128)(2,1)S(1)}, f32[4,2,1024]{2,1,0:T(2,128)S(1)}) custom-call(s32[2]{0:T(128)S(1)} %pad_add_fusion.place_ref, bf16[1024,1536]{1,0:T(8,128)(2,1)S(1)} %add_convert_fusion.mixed_ref), custom_call_target="tpu_custom_call" | custom-call | flops 2147483648 | bytes 4718592 | tf_op jit(solution)/shard_map/attend/pallas_call | solution.py:105
  106.2 5.3 all-gather.2
  122.6 5.3 collective-permute-done.21
  128.3 10.4 %collective-permute-done.20 = bf16[256,1024]{1,0:T(8,128)(2,1)S(1)} collective-permute-done((bf16[256,1024]{1,0:T(8,128)(2,1)S(1)}, bf16[256,1024]{1,0:T(8,128)(2,1)S(1)}, u32[]{:S(2)}, u32[]{:S(2)}) %collective-permute-start.20) | collective-permute-done | bytes 524320 | tf_op jit(solution)/shard_map/ppermute | solution.py:19
  142.3 8.0 %collective-permute-done.26 = bf16[1024,256]{1,0:T(8,128)(2,1)S(1)} collective-permute-done((bf16[1024,256]{1,0:T(8,128)(2,1)S(1)}, bf16[1024,256]{1,0:T(8,128)(2,1)S(1)}, u32[]{:S(2)}, u32[]{:S(2)}) %collective-permute-start.26) | collective-permute-done | bytes 524320 | tf_op jit(solution)/shard_map/ppermute | solution.py:19
  155.2 9.6 %collective-permute-done.22 = bf16[256,1024]{1,0:T(8,128)(2,1)S(1)} collective-permute-done((bf16[256,1024]{1,0:T(8,128)(2,1)S(1)}, bf16[256,1024]{1,0:T(8,128)(2,1)S(1)}, u32[]{:S(2)}, u32[]{:S(2)}) %collective-permute-start.22) | collective-permute-done | bytes 524320 | tf_op jit(solution)/shard_map/ppermute | solution.py:19
  167.9 22.3 %multiply_convert_fusion = (bf16[1024,2048]{1,0:T(8,128)(2,1)}, f32[1024,2048]{1,0:T(8,128)}) fusion(f32[2048]{0:T(1024)S(1)} %bitcast.84, bf16[256,1024]{1,0:T(8,128)(2,1)S(1)} %collective-permute-done.24, bf16[256,1024]{1,0:T(8,128)(2,1)S(1)} %collective-permute-done.23, bf16[256,1024]{1,0:T(8,128)(2,1)S(1)} %collective-permute-done.22, ...), kind=kOutput, calls=%fused_computation.8 | convolution fusion | flops 4345298944 | bytes 18882560 | tf_op jit(solution)/shard_map/dot_general | solution.py:35
  190.4 7.6 %fusion.51 = f32[1024,1024]{0,1:T(8,128)S(1)} fusion(bf16[1024,2048]{1,0:T(8,128)(2,1)} %get-tuple-element.211, bf16[1024,256]{1,0:T(8,128)(2,1)S(1)} %collective-permute-done.31, bf16[1024,256]{1,0:T(8,128)(2,1)S(1)} %collective-permute-done.30, bf16[1024,256]{1,0:T(8,128)(2,1)S(1)} %collective-permute-done.29, ...), kind=kOutput, calls=%fused_computation.200 | convolution fusion | flops 4328521728 | bytes 12582912 | tf_op jit(solution)/shard_map/dot_general | solution.py:35
  204.3 12.7 %collective-permute-done.35 = bf16[1024,256]{0,1:T(8,128)(2,1)S(1)} collective-permute-done((bf16[1024,256]{0,1:T(8,128)(2,1)}, bf16[1024,256]{0,1:T(8,128)(2,1)S(1)}, u32[]{:S(2)}, u32[]{:S(2)}) %collective-permute-start.35) | collective-permute-done | bytes 524320 | tf_op jit(solution)/shard_map/ppermute | solution.py:19
  232.1 18.3 %convert_reduce_fusion = (f32[2048]{0:T(1024)S(1)}, bf16[1024,2048]{1,0:T(8,128)(2,1)S(1)}) fusion(f32[1024,2048]{1,0:T(8,128)} %get-tuple-element.212, f32[2048]{0:T(1024)S(1)} %bitcast.85, bf16[1024,256]{1,0:T(8,128)(2,1)} %copy-done.87, bf16[1024,256]{1,0:T(8,128)(2,1)} %copy-done.86, bf16[1024,256]{1,0:T(8,128)(2,1)S(1)} %copy-done.83, ...), kind=kOutput, calls=%fused_computation.7 | convolution fusion | flops 4359976960 | bytes 18890752 | tf_op jit(solution)/shard_map/dot_general | solution.py:35
  267.9 6.8 %convolution_convert_fusion.2 = bf16[2048,1024]{1,0:T(8,128)(2,1)S(1)} fusion(bf16[1024,2048]{1,0:T(8,128)(2,1)S(1)} %copy-done.108, bf16[512,1024]{0,1:T(8,128)(2,1)} %collective-permute-done.37, bf16[512,1024]{0,1:T(8,128)(2,1)} %get-tuple-element.131), kind=kOutput, calls=%fused_computation.16 | convolution fusion | flops 4301258752 | bytes 10485760 | tf_op jit(solution)/shard_map/dot_general | solution.py:35
  280.3 10.6 %collective-permute-done.65 = bf16[1024,256]{1,0:T(8,128)(2,1)S(1)} collective-permute-done((bf16[1024,256]{1,0:T(8,128)(2,1)S(1)}, bf16[1024,256]{1,0:T(8,128)(2,1)S(1)}, u32[]{:S(2)}, u32[]{:S(2)}) %collective-permute-start.65) | collective-permute-done | bytes 524320 | tf_op jit(solution)/shard_map/ppermute | solution.py:19
  292.4 9.7 %collective-permute-done.34 = bf16[1024,256]{0,1:T(8,128)(2,1)S(1)} collective-permute-done((bf16[1024,256]{0,1:T(8,128)(2,1)S(1)}, bf16[1024,256]{0,1:T(8,128)(2,1)S(1)}, u32[]{:S(2)}, u32[]{:S(2)}) %collective-permute-start.34) | collective-permute-done | bytes 524320 | tf_op jit(solution)/shard_map/ppermute | solution.py:19
  303.0 10.4 %collective-permute-done.70 = bf16[256,1024]{1,0:T(8,128)(2,1)} collective-permute-done((bf16[256,1024]{1,0:T(8,128)(2,1)S(1)}, bf16[256,1024]{1,0:T(8,128)(2,1)}, u32[]{:S(2)}, u32[]{:S(2)}) %collective-permute-start.70) | collective-permute-done | bytes 524320 | tf_op jit(solution)/shard_map/ppermute | solution.py:19
  343.5 5.2 collective-permute-done.61
  354.5 29.1 %attend_back.1 = bf16[1024,1536]{1,0:T(8,128)(2,1)S(1)} custom-call(s32[2]{0:T(128)S(1)} %pad_add_fusion.place_ref, bf16[1024,1536]{1,0:T(8,128)(2,1)S(1)} %copy-done.3, bf16[1024,512]{1,0:T(8,128)(2,1)S(1)} %convolution_convert_fusion.4.grad_ref, f32[4,2,1024]{2,1,0:T(2,128)S(1)} %get-tuple-element.24.sums_ref), custom_call_target="tpu_custom_call" | custom-call | flops 5368709120 | bytes 7864320 | tf_op jit(solution)/shard_map/attend_back/pallas_call | solution.py:164
  385.1 6.9 %convolution_convert_fusion = bf16[1024,1536]{1,0:T(8,128)(2,1)} fusion(bf16[1024,1536]{1,0:T(8,128)(2,1)S(1)} %attend_back.1, bf16[1024,256]{0,1:T(8,128)(2,1)S(1)} %copy-done.28, bf16[1024,256]{0,1:T(8,128)(2,1)S(1)} %copy-done.22, bf16[1024,256]{0,1:T(8,128)(2,1)S(1)} %copy-done.25, bf16[1024,256]{0,1:T(8,128)(2,1)S(1)} %copy-done.19), kind=kOutput, calls=%fused_computation.14 | convolution fusion | flops 3231186944 | bytes 8388608 | tf_op jit(solution)/shard_map/dot_general | solution.py:35
  422.0 6.4 %collective-permute-done.60 = f32[2048]{0:T(1024)S(1)} collective-permute-done((f32[2048]{0:T(1024)S(1)}, f32[2048]{0:T(1024)S(1)}, u32[]{:S(2)}, u32[]{:S(2)}) %collective-permute-start.60) | collective-permute-done | bytes 8224 | tf_op jit(solution)/shard_map/ppermute | solution.py:19
  435.2 5.8 %collective-permute-done.54 = bf16[256,768]{1,0:T(8,128)(2,1)S(1)} collective-permute-done((bf16[256,768]{1,0:T(8,128)(2,1)S(1)}, bf16[256,768]{1,0:T(8,128)(2,1)S(1)}, u32[]{:S(2)}, u32[]{:S(2)}) %collective-permute-start.54) | collective-permute-done | bytes 393248 | tf_op jit(solution)/shard_map/ppermute | solution.py:19
  463.6 20.2 %all-reduce.6 = (bf16[10240]{0:T(1024)(128)(2,1)S(1)}, bf16[2,1024]{1,0:T(2,128)(2,1)S(1)}) all-reduce(bf16[10240]{0:T(1024)(128)(2,1)S(1)} %copy-done.54, bf16[2,1024]{1,0:T(2,128)(2,1)S(1)} %reshape.163), channel_id=1, replica_groups=mesh['dp'=4,'x'=2,'core'=2,'col'=2] {'dp'}, use_global_device_ids=true, to_apply=%region_25.26 | all-reduce | flops 12288 | bytes 49152 | tf_op jit(solution)/shard_map/psum | solution.py:65
  483.8 24.7 %all-reduce.12.cloned.1.call-done = (bf16[256,768]{1,0:T(8,128)(2,1)}, bf16[256,768]{1,0:T(8,128)(2,1)}, bf16[256,256]{1,0:T(8,128)(2,1)}, bf16[256,256]{1,0:T(8,128)(2,1)}) async-done(((bf16[256,768]{1,0:T(8,128)(2,1)}, bf16[256,768]{1,0:T(8,128)(2,1)}, bf16[256,256]{1,0:T(8,128)(2,1)}, bf16[256,256]{1,0:T(8,128)(2,1)}), (bf16[256,768]{1,0:T(8,128)(2,1)}, bf16[256,768]{1,0:T(8,128)(2,1)}, ...) | async-done | bytes 1048592 | tf_op jit(solution)/shard_map/psum | solution.py:65
  517.4 8.3 %collective-permute-done.42 = bf16[1024,256]{0,1:T(8,128)(2,1)S(1)} collective-permute-done((bf16[1024,256]{0,1:T(8,128)(2,1)S(1)}, bf16[1024,256]{0,1:T(8,128)(2,1)S(1)}, u32[]{:S(2)}, u32[]{:S(2)}) %collective-permute-start.42) | collective-permute-done | bytes 524320 | tf_op jit(solution)/shard_map/ppermute | solution.py:19
  (526 shorter events, 225.0 us)
Async XLA Ops:
  7.2 437.5 %all-reduce.14.cloned.1.call-start = ((), (), s32[]{:S(2)}) async-start(), calls=%async_computation.1 | async-start | bytes 4194304 | tf_op jit(solution)/shard_map/psum | solution.py:65
  34.7 24.8 %collective-permute-start.3 = (bf16[256,768]{1,0:T(8,128)(2,1)S(1)}, bf16[256,768]{1,0:T(8,128)(2,1)S(1)}, u32[]{:S(2)}, u32[]{:S(2)}) collective-permute-start(bf16[256,768]{1,0:T(8,128)(2,1)S(1)} %get-tuple-element.153), channel_id=1, source_target_pairs={{0,1},{1,0},{2,3},{3,2},{4,5},{5,4},{6,7},{7,6},{8,9},{9,8},{10,11... | collective-permute-start | bytes 1179656 | tf_op jit(solution)/shard_map/ppermute | solution.py:19
  59.3 38.9 %collective-permute-start.11 = (bf16[256,256]{1,0:T(8,128)(2,1)S(1)}, bf16[256,256]{1,0:T(8,128)(2,1)S(1)}, u32[]{:S(2)}, u32[]{:S(2)}) collective-permute-start(bf16[256,256]{1,0:T(8,128)(2,1)S(1)} %get-tuple-element.192), channel_id=1, source_target_pairs={{0,4},{4,0},{1,5},{5,1},{2,6},{6,2},{3,7},{7,3},{8,12},{12,8},{9,1... | collective-permute-start | bytes 393224 | tf_op jit(solution)/shard_map/ppermute | solution.py:19
  59.6 38.6 %collective-permute-start.12 = (bf16[256,256]{1,0:T(8,128)(2,1)S(1)}, bf16[256,256]{1,0:T(8,128)(2,1)S(1)}, u32[]{:S(2)}, u32[]{:S(2)}) collective-permute-start(bf16[256,256]{1,0:T(8,128)(2,1)S(1)} %get-tuple-element.191), channel_id=1, source_target_pairs={{0,1},{1,0},{2,3},{3,2},{4,5},{5,4},{6,7},{7,6},{8,9},{9,8},{10,11... | collective-permute-start | bytes 393224 | tf_op jit(solution)/shard_map/ppermute | solution.py:19
  61.3 36.8 %collective-permute-start.14 = (bf16[256,256]{1,0:T(8,128)(2,1)S(1)}, bf16[256,256]{1,0:T(8,128)(2,1)S(1)}, u32[]{:S(2)}, u32[]{:S(2)}) collective-permute-start(bf16[256,256]{1,0:T(8,128)(2,1)S(1)} %collective-permute-done.10), channel_id=1, source_target_pairs={{0,1},{1,0},{2,3},{3,2},{4,5},{5,4},{6,7},{7,6},{8,9},{9,8},{10,11... | collective-permute-start | bytes 393224 | tf_op jit(solution)/shard_map/ppermute | solution.py:19
  61.6 36.6 %collective-permute-start.15 = (bf16[256,256]{1,0:T(8,128)(2,1)S(1)}, bf16[256,256]{1,0:T(8,128)(2,1)S(1)}, u32[]{:S(2)}, u32[]{:S(2)}) collective-permute-start(bf16[256,256]{1,0:T(8,128)(2,1)S(1)} %collective-permute-done.13), channel_id=1, source_target_pairs={{0,4},{4,0},{1,5},{5,1},{2,6},{6,2},{3,7},{7,3},{8,12},{12,8},{9,1... | collective-permute-start | bytes 393224 | tf_op jit(solution)/shard_map/ppermute | solution.py:19
  113.6 26.7 %collective-permute-start.19 = (bf16[256,1024]{1,0:T(8,128)(2,1)S(1)}, bf16[256,1024]{1,0:T(8,128)(2,1)S(1)}, u32[]{:S(2)}, u32[]{:S(2)}) collective-permute-start(bf16[256,1024]{1,0:T(8,128)(2,1)S(1)} %get-tuple-element.151), channel_id=1, source_target_pairs={{0,1},{1,0},{2,3},{3,2},{4,5},{5,4},{6,7},{7,6},{8,9},{9,8},{10,11... | collective-permute-start | bytes 1572872 | tf_op jit(solution)/shard_map/ppermute | solution.py:19
  115.6 25.1 %collective-permute-start.23 = (bf16[256,1024]{1,0:T(8,128)(2,1)S(1)}, bf16[256,1024]{1,0:T(8,128)(2,1)S(1)}, u32[]{:S(2)}, u32[]{:S(2)}) collective-permute-start(bf16[256,1024]{1,0:T(8,128)(2,1)S(1)} %get-tuple-element.152), channel_id=1, source_target_pairs={{0,4},{4,0},{1,5},{5,1},{2,6},{6,2},{3,7},{7,3},{8,12},{12,8},{9,1... | collective-permute-start | bytes 1572872 | tf_op jit(solution)/shard_map/ppermute | solution.py:19
  120.5 47.4 %collective-permute-start.17 = (bf16[512,1024]{0,1:T(8,128)(2,1)S(1)}, bf16[512,1024]{0,1:T(8,128)(2,1)S(1)}, u32[]{:S(2)}, u32[]{:S(2)}) collective-permute-start(bf16[512,1024]{0,1:T(8,128)(2,1)S(1)} %fusion.19), channel_id=1, source_target_pairs={{0,2},{2,0},{1,3},{3,1},{4,6},{6,4},{5,7},{7,5},{8,10},{10,8},{9,1... | collective-permute-start | bytes 3145736 | tf_op jit(solution)/shard_map/ppermute | solution.py:19
  140.3 24.5 %collective-permute-start.22 = (bf16[256,1024]{1,0:T(8,128)(2,1)S(1)}, bf16[256,1024]{1,0:T(8,128)(2,1)S(1)}, u32[]{:S(2)}, u32[]{:S(2)}) collective-permute-start(bf16[256,1024]{1,0:T(8,128)(2,1)S(1)} %collective-permute-done.21), channel_id=1, source_target_pairs={{0,1},{1,0},{2,3},{3,2},{4,5},{5,4},{6,7},{7,6},{8,9},{9,8},{10,11... | collective-permute-start | bytes 1572872 | tf_op jit(solution)/shard_map/ppermute | solution.py:19
  140.7 25.7 %collective-permute-start.24 = (bf16[256,1024]{1,0:T(8,128)(2,1)S(1)}, bf16[256,1024]{1,0:T(8,128)(2,1)S(1)}, u32[]{:S(2)}, u32[]{:S(2)}) collective-permute-start(bf16[256,1024]{1,0:T(8,128)(2,1)S(1)} %collective-permute-done.20), channel_id=1, source_target_pairs={{0,4},{4,0},{1,5},{5,1},{2,6},{6,2},{3,7},{7,3},{8,12},{12,8},{9,1... | collective-permute-start | bytes 1572872 | tf_op jit(solution)/shard_map/ppermute | solution.py:19
  150.4 39.9 %collective-permute-start.27 = (bf16[1024,256]{1,0:T(8,128)(2,1)S(1)}, bf16[1024,256]{1,0:T(8,128)(2,1)S(1)}, u32[]{:S(2)}, u32[]{:S(2)}) collective-permute-start(bf16[1024,256]{1,0:T(8,128)(2,1)S(1)} %get-tuple-element.150), channel_id=1, source_target_pairs={{0,4},{4,0},{1,5},{5,1},{2,6},{6,2},{3,7},{7,3},{8,12},{12,8},{9,1... | collective-permute-start | bytes 1572872 | tf_op jit(solution)/shard_map/ppermute | solution.py:19
  153.6 36.7 %collective-permute-start.28 = (bf16[1024,256]{1,0:T(8,128)(2,1)S(1)}, bf16[1024,256]{1,0:T(8,128)(2,1)S(1)}, u32[]{:S(2)}, u32[]{:S(2)}) collective-permute-start(bf16[1024,256]{1,0:T(8,128)(2,1)S(1)} %get-tuple-element.149), channel_id=1, source_target_pairs={{0,1},{1,0},{2,3},{3,2},{4,5},{5,4},{6,7},{7,6},{8,9},{9,8},{10,11... | collective-permute-start | bytes 1572872 | tf_op jit(solution)/shard_map/ppermute | solution.py:19
  164.8 25.5 %collective-permute-start.30 = (bf16[1024,256]{1,0:T(8,128)(2,1)S(1)}, bf16[1024,256]{1,0:T(8,128)(2,1)S(1)}, u32[]{:S(2)}, u32[]{:S(2)}) collective-permute-start(bf16[1024,256]{1,0:T(8,128)(2,1)S(1)} %collective-permute-done.26), channel_id=1, source_target_pairs={{0,1},{1,0},{2,3},{3,2},{4,5},{5,4},{6,7},{7,6},{8,9},{9,8},{10,11... | collective-permute-start | bytes 1572872 | tf_op jit(solution)/shard_map/ppermute | solution.py:19
  266.7 65.4 %collective-permute-start.38 = (f32[512,1024]{0,1:T(8,128)}, f32[512,1024]{0,1:T(8,128)}, u32[]{:S(2)}, u32[]{:S(2)}) collective-permute-start(f32[512,1024]{0,1:T(8,128)} %slice.341), channel_id=1, source_target_pairs={{0,2},{2,0},{1,3},{3,1},{4,6},{6,4},{5,7},{7,5},{8,10},{10,8},{9,1... | collective-permute-start | bytes 6291464 | tf_op jit(solution)/shard_map/ppermute | solution.py:19
  276.7 25.4 %collective-permute-start.34 = (bf16[1024,256]{0,1:T(8,128)(2,1)S(1)}, bf16[1024,256]{0,1:T(8,128)(2,1)S(1)}, u32[]{:S(2)}, u32[]{:S(2)}) collective-permute-start(bf16[1024,256]{0,1:T(8,128)(2,1)S(1)} %get-tuple-element.168), channel_id=1, source_target_pairs={{0,4},{4,0},{1,5},{5,1},{2,6},{6,2},{3,7},{7,3},{8,12},{12,8},{9,1... | collective-permute-start | bytes 1572872 | tf_op jit(solution)/shard_map/ppermute | solution.py:19
  278.7 34.6 %collective-permute-start.70 = (bf16[256,1024]{1,0:T(8,128)(2,1)S(1)}, bf16[256,1024]{1,0:T(8,128)(2,1)}, u32[]{:S(2)}, u32[]{:S(2)}) collective-permute-start(bf16[256,1024]{1,0:T(8,128)(2,1)S(1)} %get-tuple-element.121), channel_id=1, source_target_pairs={{0,4},{4,0},{1,5},{5,1},{2,6},{6,2},{3,7},{7,3},{8,12},{12,8},{9,1... | collective-permute-start | bytes 1572872 | tf_op jit(solution)/shard_map/ppermute | solution.py:19
  290.8 26.7 %collective-permute-start.72 = (bf16[256,1024]{1,0:T(8,128)(2,1)}, bf16[256,1024]{1,0:T(8,128)(2,1)}, u32[]{:S(2)}, u32[]{:S(2)}) collective-permute-start(bf16[256,1024]{1,0:T(8,128)(2,1)} %add_convert_fusion.3), channel_id=1, source_target_pairs={{0,1},{1,0},{2,3},{3,2},{4,5},{5,4},{6,7},{7,6},{8,9},{9,8},{10,11... | collective-permute-start | bytes 1572872 | tf_op jit(solution)/shard_map/ppermute | solution.py:19
  322.4 26.3 %collective-permute-start.61 = (bf16[1024,256]{1,0:T(8,128)(2,1)}, bf16[1024,256]{1,0:T(8,128)(2,1)}, u32[]{:S(2)}, u32[]{:S(2)}) collective-permute-start(bf16[1024,256]{1,0:T(8,128)(2,1)} %get-tuple-element.130), channel_id=1, source_target_pairs={{0,1},{1,0},{2,3},{3,2},{4,5},{5,4},{6,7},{7,6},{8,9},{9,8},{10,11... | collective-permute-start | bytes 1572872 | tf_op jit(solution)/shard_map/ppermute | solution.py:19
  351.5 156.9 %all-reduce.12.cloned.1.call-start = ((), (), s32[]{:S(2)}) async-start(), calls=%async_computation | async-start | bytes 2097152 | tf_op jit(solution)/shard_map/psum | solution.py:65
  352.2 56.8 %collective-permute-start.57 = (f32[10240]{0:T(1024)}, f32[10240]{0:T(1024)}, u32[]{:S(2)}, u32[]{:S(2)}) collective-permute-start(f32[10240]{0:T(1024)} %add.383), channel_id=1, source_target_pairs={{0,1},{1,0},{2,3},{3,2},{4,5},{5,4},{6,7},{7,6},{8,9},{9,8},{10,11... | collective-permute-start | bytes 122888 | tf_op jit(solution)/shard_map/ppermute | solution.py:19
  394.1 26.5 %collective-permute-start.53 = (bf16[256,768]{1,0:T(8,128)(2,1)S(1)}, bf16[256,768]{1,0:T(8,128)(2,1)S(1)}, u32[]{:S(2)}, u32[]{:S(2)}) collective-permute-start(bf16[256,768]{1,0:T(8,128)(2,1)S(1)} %get-tuple-element.135), channel_id=1, source_target_pairs={{0,4},{4,0},{1,5},{5,1},{2,6},{6,2},{3,7},{7,3},{8,12},{12,8},{9,1... | collective-permute-start | bytes 1179656 | tf_op jit(solution)/shard_map/ppermute | solution.py:19
  409.0 44.5 %collective-permute-start.40 = (f32[512,1024]{0,1:T(8,128)}, f32[512,1024]{0,1:T(8,128)}, u32[]{:S(2)}, u32[]{:S(2)}) collective-permute-start(f32[512,1024]{0,1:T(8,128)} %slice.343), channel_id=1, source_target_pairs={{0,2},{2,0},{1,3},{3,1},{4,6},{6,4},{5,7},{7,5},{8,10},{10,8},{9,1... | collective-permute-start | bytes 6291464 | tf_op jit(solution)/shard_map/ppermute | solution.py:19
  457.9 53.4 %collective-permute-start.41 = (f32[512,512]{0,1:T(8,128)}, f32[512,512]{0,1:T(8,128)S(1)}, u32[]{:S(2)}, u32[]{:S(2)}) collective-permute-start(f32[512,512]{0,1:T(8,128)} %get-tuple-element.140), channel_id=1, source_target_pairs={{0,2},{2,0},{1,3},{3,1},{4,6},{6,4},{5,7},{7,5},{8,10},{10,8},{9,1... | collective-permute-start | bytes 3145736 | tf_op jit(solution)/shard_map/ppermute | solution.py:19
  (166 other events, 2356.4 us)
Sparse Core Ops, SparseCore 0:
  351.6 87.4 all-reduce.13
  453.6 54.7 all-reduce.11
